TPU v7x, 32 devices: a whole 2x2x4 slice. The times are simulated.
32 devices in a mesh: groups: 2 (over y), ctx: 4 (over z), head: 2 (over x), pair: 2 (over core).
Axes of the slice: x: 2, y: 2, z: 4, core: 2. Of those that a mesh axis runs over, the one named last changes fastest.
Arguments:
- student_query: bfloat16 [1024, 4096], P(('groups', 'ctx'), ('head', 'pair')), parts along dimension 0, may hold values from -25 to 25
- teacher_keys: bfloat16 [1024, 1024], P(('groups', 'ctx'), ('head', 'pair')), parts along dimension 0, may hold values from -9 to 9
- teacher_values: bfloat16 [1024, 1024], P(('groups', 'ctx'), ('head', 'pair')), parts along dimension 0, may hold values from -6 to 6
- band_span: int32 [1024], P(('groups', 'ctx')), parts along dimension 0, may hold values from 256 to 1024, as said below
- residual_in: bfloat16 [1024, 4096], P(('groups', 'ctx'), ('head', 'pair')), parts along dimension 0, may hold values from -3 to 3
- norm_gain: float32 [4096], replicated, may hold values from 0.25 to 1.75
- w_gate: bfloat16 [4096, 7168], P('ctx', ('head', 'pair')), may hold values from -0.09375 to 0.09375
- w_up: bfloat16 [4096, 7168], P('ctx', ('head', 'pair')), may hold values from -0.09375 to 0.09375
- w_down: bfloat16 [7168, 4096], P(('head', 'pair'), 'ctx'), may hold values from -0.0625 to 0.0625
- teacher_feats: bfloat16 [1024, 7168], P(('groups', 'ctx'), ('head', 'pair')), parts along dimension 0, may hold values from -31 to 31
- keep_tiles: int32 [1024, 56], P(('groups', 'ctx'), ('head', 'pair')), parts along dimension 0, may hold values from 0 to 1, as said below
Outputs:
- layer_out: bfloat16 [1024, 4096], P(('groups', 'ctx'), ('head', 'pair')), parts along dimension 0
- loss_value: float32 [2], P('groups'), parts along dimension 0
- grad_resid: float32 [1024, 4096], P(('groups', 'ctx'), ('head', 'pair')), parts along dimension 0
There are 2 independent parts, one for each index of `groups`. A program takes and returns all parts, laid end to end along the dimension named above; an argument that names none is the same for every part. Nothing has to cross between parts.
Inputs may be any that keep to these rules, and one draw needn't show every extreme that they name: `band_span`: some token's span equals 1024. `keep_tiles`: the first token keeps every tile.
All inputs are finite; a program needn't handle non-finite values.
Results may differ from a plain program's by a relative error of at most 0.014.
Values may be sent and summed in bfloat16 or wider, within the bound.
A program may use at most 128 MiB of HBM per device.

v0:
```python
import math

import jax
import jax.numpy as jnp
from jax import lax
from jax.sharding import PartitionSpec as P

D = 4096
HEADS = 32
KV_HEADS = 8
HEAD_DIM = 128
TILE = 128
BAND = 8


def passed_along(block, axis, distance):
    devices = range(lax.axis_size(axis))
    route = [(i - distance, i) for i in devices if i - distance in devices]
    return lax.ppermute(block, axis, route)


def attend_heads(query_part, key_rows, value_rows, allowed):
    scores = jnp.einsum("thd,sd->hts", query_part, key_rows, preferred_element_type=jnp.float32) * (
        1.0 / math.sqrt(HEAD_DIM)
    )
    masked = jnp.where(allowed[None], scores, -jnp.inf)
    highest = jnp.max(masked, axis=-1, keepdims=True)
    weights = jnp.exp(masked - highest)
    normalized = (weights / jnp.sum(weights, axis=-1, keepdims=True)).astype(jnp.bfloat16)
    return jnp.einsum("hts,sd->thd", normalized, value_rows, preferred_element_type=jnp.float32)


def local(
    student_query,
    teacher_keys,
    teacher_values,
    band_span,
    residual_in,
    norm_gain,
    w_gate,
    w_up,
    w_down,
    teacher_feats,
    keep_tiles,
):
    tok_rows = student_query.shape[0]
    kv_local = teacher_keys.shape[1] // HEAD_DIM
    group_size = HEADS // KV_HEADS
    ctx_index = lax.axis_index("ctx")
    paired = jnp.stack([teacher_keys, teacher_values])

    def pass_block(carried, unused_step):
        moved = passed_along(carried, "ctx", 1)
        return (moved, moved)

    unused_last, earlier = lax.scan(pass_block, paired, None, length=BAND)
    all_blocks = jnp.concatenate([paired[None], earlier], axis=0)
    rounds_count = BAND + 1
    round_ids = jnp.arange(rounds_count, dtype=jnp.int32)
    key_pos = (
        (ctx_index - round_ids)[:, None] * tok_rows + jnp.arange(tok_rows, dtype=jnp.int32)[None, :]
    ).reshape(-1)
    query_pos = ctx_index * tok_rows + jnp.arange(tok_rows, dtype=jnp.int32)
    distance = query_pos[:, None] - key_pos[None, :]
    allowed = (distance >= 0) & (distance < band_span[:, None]) & (key_pos[None, :] >= 0)
    keys_flat = all_blocks[:, 0].reshape(rounds_count * tok_rows, kv_local, HEAD_DIM)
    values_flat = all_blocks[:, 1].reshape(rounds_count * tok_rows, kv_local, HEAD_DIM)
    query_heads = student_query.reshape(tok_rows, kv_local, group_size, HEAD_DIM)
    outputs = []
    for kv_head in range(kv_local):
        for first_head in range(0, group_size, 2):
            outputs.append(
                attend_heads(
                    query_heads[:, kv_head, first_head : first_head + 2],
                    keys_flat[:, kv_head],
                    values_flat[:, kv_head],
                    allowed,
                )
            )
    attended = jnp.concatenate(outputs, axis=1).reshape(tok_rows, -1)
    residual = (residual_in.astype(jnp.float32) + attended).astype(jnp.bfloat16)
    gathered = lax.all_gather(residual, ("head", "pair"), axis=1, tiled=True)
    full_float = gathered.astype(jnp.float32)
    rms_value = jnp.sqrt(jnp.mean(full_float * full_float, axis=1, keepdims=True) + 1e-05)
    normed = (full_float / rms_value * norm_gain).astype(jnp.bfloat16)
    gate_full, up_full = (
        lax.all_gather(w_gate, "ctx", axis=0, tiled=True),
        lax.all_gather(w_up, "ctx", axis=0, tiled=True),
    )
    gate_proj = jnp.dot(normed, gate_full, preferred_element_type=jnp.float32)
    up_proj = jnp.dot(normed, up_full, preferred_element_type=jnp.float32)
    lifted = jnp.maximum(gate_proj, 0.0)
    squared = lifted * lifted
    act_value = squared * up_proj
    hidden = act_value.astype(jnp.bfloat16)
    all_hidden = lax.all_gather(hidden, "ctx", axis=0, tiled=True)
    local_part = jnp.dot(all_hidden, w_down, preferred_element_type=jnp.float32).astype(
        jnp.bfloat16
    )
    routed = lax.all_to_all(local_part, "ctx", split_axis=0, concat_axis=1, tiled=True)
    down_sum = lax.psum_scatter(
        routed.astype(jnp.float32).astype(jnp.bfloat16),
        ("head", "pair"),
        scatter_dimension=1,
        tiled=True,
    ).astype(jnp.float32)
    resid_own = residual.astype(jnp.float32)
    layer_out = (resid_own + down_sum).astype(jnp.bfloat16)
    tile_count = keep_tiles.shape[1]
    keep_float = keep_tiles.astype(jnp.float32)
    keep_wide = jnp.broadcast_to(keep_float[:, :, None], (tok_rows, tile_count, TILE)).reshape(
        tok_rows, tile_count * TILE
    )
    differ = act_value - teacher_feats.astype(jnp.float32)
    loss_part = jnp.sum(keep_wide * differ * differ)
    count_part = jnp.sum(keep_float) * TILE
    loss_total, count_total = lax.psum((loss_part, count_part), ("ctx", "head", "pair"))
    loss_value = (loss_total / count_total).reshape(1)
    grad_act = keep_wide * differ
    grad_gate = (grad_act * up_proj * 2.0 * lifted).astype(jnp.bfloat16)
    grad_up = (grad_act * squared).astype(jnp.bfloat16)
    contract = (((1,), (1,)), ((), ()))
    grad_part = lax.dot_general(grad_gate, gate_full, contract, preferred_element_type=jnp.float32)
    grad_part = grad_part + lax.dot_general(
        grad_up, up_full, contract, preferred_element_type=jnp.float32
    )
    own_cols = residual.shape[1]
    own_start = lax.axis_index(("head", "pair")) * own_cols
    gain_own = lax.dynamic_slice_in_dim(norm_gain, own_start, own_cols, 0)
    rms_cubed = rms_value * rms_value * rms_value
    grad_norm = lax.psum_scatter(
        grad_part.astype(jnp.bfloat16), ("head", "pair"), scatter_dimension=1, tiled=True
    ).astype(jnp.float32)
    inner_sum = lax.psum(
        jnp.sum(gain_own * grad_norm * resid_own, axis=1, keepdims=True), ("head", "pair")
    )
    grad_resid = gain_own * grad_norm / rms_value - resid_own * inner_sum / (D * rms_cubed)
    return (layer_out, loss_value, grad_resid)


def solution(mesh):
    in_specs = (
        P(("groups", "ctx"), ("head", "pair")),
        P(("groups", "ctx"), ("head", "pair")),
        P(("groups", "ctx"), ("head", "pair")),
        P(("groups", "ctx")),
        P(("groups", "ctx"), ("head", "pair")),
        P(),
        P("ctx", ("head", "pair")),
        P("ctx", ("head", "pair")),
        P(("head", "pair"), "ctx"),
        P(("groups", "ctx"), ("head", "pair")),
        P(("groups", "ctx"), ("head", "pair")),
    )
    out_specs = (
        P(("groups", "ctx"), ("head", "pair")),
        P("groups"),
        P(("groups", "ctx"), ("head", "pair")),
    )
    return jax.shard_map(local, mesh=mesh, in_specs=in_specs, out_specs=out_specs, check_vma=False)
```

profile of v0, /device:TPU:0, one launch (start us, length us, event | category | flops | bytes accessed | tf_op | source)
XLA Modules:
  0.0 737.7 jit_solution(9024494652574293018)
XLA Ops:
  7.4 0.9 fusion.71
  8.3 57.8 %while.12 = (s32[]{:T(128)}, bf16[2,128,256]{2,1,0:T(8,128)(2,1)S(1)}, bf16[8,2,128,256]{3,2,1,0:T(8,128)(2,1)S(1)}, s32[]{:T(128)}) while((s32[]{:T(128)}, bf16[2,128,256]{2,1,0:T(8,128)(2,1)S(1)}, bf16[8,2,128,256]{3,2,1,0:T(8,128)(2,1)S(1)}, s32[]{:T(128)}) %tuple.30), condition=%wide.region_1.2_spmd, body=%wide.region_0.1_spmd.sunk | while | flops 2 | bytes 1048681 | solution.py:56
  8.3 4.9 collective-permute-start
  13.2 2.7 collective-permute-done
  16.0 4.4 collective-permute-start
  20.4 2.5 collective-permute-done
  23.0 4.4 collective-permute-start
  27.3 2.5 collective-permute-done
  29.9 4.4 collective-permute-start
  34.2 2.5 collective-permute-done
  36.8 4.4 collective-permute-start
  41.2 3.6 collective-permute-done
  44.8 4.4 collective-permute-start
  49.2 3.0 collective-permute-done
  52.2 4.4 collective-permute-start
  56.6 2.5 collective-permute-done
  59.2 4.4 collective-permute-start
  63.6 2.5 collective-permute-done
  66.4 0.9 fusion.76
  67.5 0.9 fusion.27
  69.6 0.6 fusion.78
  70.9 0.9 fusion.75
  71.8 0.6 copy.42
  72.4 0.8 convolution_bitcast_fusion.3
  73.3 0.8 convolution_bitcast_fusion.2
  74.1 0.6 copy.46
  74.7 0.8 convolution_bitcast_fusion.1
  75.5 0.8 convolution_bitcast_fusion
  76.6 0.7 copy-done.5
  77.3 0.8 add_convert_fusion
  78.1 0.7 all-gather.7.cloned.1.call-update
  78.9 0.7 all-gather.9.cloned.1.call-update
  80.2 16.9 %all-gather.5.cloned.1.call-done = bf16[128,4096]{1,0:T(8,128)(2,1)} async-done(((bf16[128,1024]{1,0:T(8,128)(2,1)}), bf16[128,4096]{1,0:T(8,128)(2,1)}) %all-gather.5.cloned.1.call-update) | async-done | bytes 1048592 | tf_op jit(solution)/shard_map/all_gather | solution.py:82
  97.0 1.5 fusion.21
  98.6 252.6 %all-gather.7.cloned.1.call-done = bf16[4096,1792]{1,0:T(8,128)(2,1)} async-done(((bf16[1024,1792]{1,0:T(8,128)(2,1)}), bf16[4096,1792]{1,0:T(8,128)(2,1)}) %all-gather.7.cloned.1.call-update) | async-done | bytes 14680080 | tf_op jit(solution)/shard_map/all_gather | solution.py:87
  351.2 7.7 %convolution_maximum_fusion = f32[128,1792]{1,0:T(8,128)S(1)} fusion(bf16[4096,1792]{1,0:T(8,128)(2,1)} %all-gather.7.cloned.1.call-done, bf16[128,4096]{1,0:T(8,128)(2,1)} %all-gather.5.cloned.1.call-done, f32[4096]{0:T(1024)S(1)} %copy-done.7, f32[128]{0:T(128)S(1)} %get-tuple-element.42), kind=kOutput, calls=%fused_computation.29 | convolution fusion | flops 1881374720 | bytes 16663040 | tf_op jit(solution)/shard_map/dot_general | solution.py:90
  358.9 244.5 %all-gather.9.cloned.1.call-done = bf16[4096,1792]{1,0:T(8,128)(2,1)} async-done(((bf16[1024,1792]{1,0:T(8,128)(2,1)}), bf16[4096,1792]{1,0:T(8,128)(2,1)}) %all-gather.9.cloned.1.call-update) | async-done | bytes 14680080 | tf_op jit(solution)/shard_map/all_gather | solution.py:88
  603.4 9.0 %multiply_reduce_fusion = (f32[]{:T(128)}, bf16[128,1792]{1,0:T(8,128)(2,1)}, f32[128,1792]{1,0:T(8,128)}) fusion(bf16[128,1792]{1,0:T(8,128)(2,1)S(1)} %copy-done.2, f32[128,1792]{1,0:T(8,128)S(1)} %copy.37, f32[128,1792]{1,0:T(8,128)S(1)} %convolution_maximum_fusion, bf16[4096,1792]{1,0:T(8,128)(2,1)} %all-gather.9.cloned.1.call-done, ...), kind=kOutput, calls=%fused_computation.46 | convolution fusion | flops 1882980352 | bytes 19415556 | tf_op jit(solution)/shard_map/dot_general | solution.py:91
  612.5 10.7 %fusion.32 = f32[128,4096]{1,0:T(8,128)S(1)} fusion(bf16[4096,1792]{1,0:T(8,128)(2,1)} %all-gather.7.cloned.1.call-done, f32[128,1792]{1,0:T(8,128)} %copy-done.1, f32[128,1792]{1,0:T(8,128)} %get-tuple-element.43, f32[128,1792]{1,0:T(8,128)S(1)} %copy.37, bf16[128,1792]{1,0:T(8,128)(2,1)S(1)} %copy-done.2), kind=kOutput, calls=%fused_computation.66 | convolution fusion | flops 1881112576 | bytes 19988480 | tf_op jit(solution)/shard_map/dot_general | solution.py:123
  623.3 11.6 %fusion.4 = bf16[128,4096]{1,0:T(8,128)(2,1)} fusion(f32[128,4096]{1,0:T(8,128)S(1)} %fusion.32, bf16[4096,1792]{1,0:T(8,128)(2,1)} %all-gather.9.cloned.1.call-done, f32[128,1792]{1,0:T(8,128)} %copy-done.1, f32[128,1792]{1,0:T(8,128)S(1)} %copy.37, bf16[128,1792]{1,0:T(8,128)(2,1)S(1)} %copy-done.2, f32[128,1792]{1,0:T(8,128)} %get-tuple-element.43), kind=kOutput, calls=%fused_computation.6 | convolution fusion | flops 1881702400 | bytes 21037056 | tf_op jit(solution)/shard_map/dot_general | solution.py:124
  635.0 17.2 %all-gather.11.cloned.1.call-done = bf16[512,1792]{1,0:T(8,128)(2,1)} async-done(((bf16[128,1792]{1,0:T(8,128)(2,1)}), bf16[512,1792]{1,0:T(8,128)(2,1)}) %all-gather.11.cloned.1.call-update) | async-done | bytes 1835024 | tf_op jit(solution)/shard_map/all_gather | solution.py:96
  652.2 4.7 convolution_convert_fusion
  656.9 28.4 %all_to_all.19 = bf16[4,128,1024]{2,1,0:T(8,128)(2,1)S(1)} all-to-all(bf16[4,128,1024]{2,1,0:T(8,128)(2,1)S(1)} %bitcast.216), channel_id=1, replica_groups=mesh['groups'=2,'ctx'=4,'head'=2,'pair'=2] {'ctx'}, dimensions={0} | all-to-all | bytes 2097152 | tf_op jit(solution)/shard_map/all_to_all | solution.py:100
  685.3 1.1 copy.50
  687.7 31.7 %all-reduce = (f32[]{:T(128)}, f32[]{:T(128)}) all-reduce(f32[]{:T(128)} %get-tuple-element.29, f32[]{:T(128)S(6)} %mul.149), channel_id=1, replica_groups=mesh['groups'=2,'ctx'=4,'head'=2,'pair'=2] {'ctx','head','pair'}, use_global_device_ids=true, to_apply=%region_13.14 | all-reduce | flops 2 | bytes 16 | tf_op jit(solution)/shard_map/psum | solution.py:117
  720.8 1.1 fusion.29
  721.9 5.8 psum.23
  727.6 2.1 fusion.31
  (65 shorter events, 4.5 us)
Async XLA Ops:
  7.2 89.9 %all-gather.5.cloned.1.call-start = ((), (), s32[]{:S(2)}) async-start(), calls=%async_computation.3 | async-start | bytes 1310720 | tf_op jit(solution)/shard_map/all_gather | solution.py:82
  8.3 7.7 %collective-permute-start = (bf16[2,128,256]{2,1,0:T(8,128)(2,1)S(1)}, bf16[2,128,256]{2,1,0:T(8,128)(2,1)S(1)}, u32[]{:S(2)}, u32[]{:S(2)}) collective-permute-start(bf16[2,128,256]{2,1,0:T(8,128)(2,1)S(1)} %get-tuple-element.68), channel_id=1, source_target_pairs={{0,4},{4,8},{8,12},{1,5},{5,9},{9,13},{2,6},{6,10},{10,14},{3,7},{... | collective-permute-start | bytes 393224 | tf_op jit(solution)/shard_map/while/body/eval_jaxpr/ppermute | solution.py:19
  16.0 6.9 collective-permute-start
  23.0 6.9 collective-permute-start
  29.9 6.9 collective-permute-start
  36.8 7.9 %collective-permute-start = (bf16[2,128,256]{2,1,0:T(8,128)(2,1)S(1)}, bf16[2,128,256]{2,1,0:T(8,128)(2,1)S(1)}, u32[]{:S(2)}, u32[]{:S(2)}) collective-permute-start(bf16[2,128,256]{2,1,0:T(8,128)(2,1)S(1)} %get-tuple-element.68), channel_id=1, source_target_pairs={{0,4},{4,8},{8,12},{1,5},{5,9},{9,13},{2,6},{6,10},{10,14},{3,7},{... | collective-permute-start | bytes 393224 | tf_op jit(solution)/shard_map/while/body/eval_jaxpr/ppermute | solution.py:19
  44.8 7.4 %collective-permute-start = (bf16[2,128,256]{2,1,0:T(8,128)(2,1)S(1)}, bf16[2,128,256]{2,1,0:T(8,128)(2,1)S(1)}, u32[]{:S(2)}, u32[]{:S(2)}) collective-permute-start(bf16[2,128,256]{2,1,0:T(8,128)(2,1)S(1)} %get-tuple-element.68), channel_id=1, source_target_pairs={{0,4},{4,8},{8,12},{1,5},{5,9},{9,13},{2,6},{6,10},{10,14},{3,7},{... | collective-permute-start | bytes 393224 | tf_op jit(solution)/shard_map/while/body/eval_jaxpr/ppermute | solution.py:19
  52.2 6.9 collective-permute-start
  59.2 6.9 collective-permute-start
  66.4 1.0 copy-start.4
  66.4 1.1 copy-start.8
  76.3 1.0 copy-start.5
  78.1 273.1 %all-gather.7.cloned.1.call-start = ((), (), s32[]{:S(2)}) async-start(), calls=%async_computation.4 | async-start | bytes 18350080 | tf_op jit(solution)/shard_map/all_gather | solution.py:87
  78.8 1.0 copy-start.6
  78.8 524.6 %all-gather.9.cloned.1.call-start = ((), (), s32[]{:S(2)}) async-start(), calls=%async_computation.5 | async-start | bytes 18350080 | tf_op jit(solution)/shard_map/all_gather | solution.py:88
  79.6 572.7 %all-gather.11.cloned.1.call-start = ((), (), s32[]{:S(2)}) async-start(), calls=%async_computation.6 | async-start | bytes 2293760 | tf_op jit(solution)/shard_map/all_gather | solution.py:96
  79.9 271.3 %copy-start.7 = (f32[4096]{0:T(1024)S(1)}, f32[4096]{0:T(1024)}, u32[]{:S(2)}) copy-start(f32[4096]{0:T(1024)} %param.18) | copy-start | bytes 49156
  351.1 252.3 %copy-start.2 = (bf16[128,1792]{1,0:T(8,128)(2,1)S(1)}, bf16[128,1792]{1,0:T(8,128)(2,1)}, u32[]{:S(2)}) copy-start(bf16[128,1792]{1,0:T(8,128)(2,1)} %param.22) | copy-start | bytes 1376260
  351.2 252.3 %copy-start.3 = (bf16[128,4096]{1,0:T(8,128)(2,1)S(1)}, bf16[128,4096]{1,0:T(8,128)(2,1)}, u32[]{:S(2)}) copy-start(bf16[128,4096]{1,0:T(8,128)(2,1)} %all-gather.5.cloned.1.call-done) | copy-start | bytes 3145732
  358.9 253.6 %copy-start.1 = (f32[128,1792]{1,0:T(8,128)}, f32[128,1792]{1,0:T(8,128)S(1)}, u32[]{:S(2)}) copy-start(f32[128,1792]{1,0:T(8,128)S(1)} %convolution_maximum_fusion) | copy-start | bytes 2752516
  612.5 108.2 %reduce-scatter.5.cloned.1.call-start = ((), (), s32[]{:S(2)}) async-start(), calls=%async_computation.8 | async-start | bytes 1310720 | tf_op jit(solution)/shard_map/reduce_scatter | solution.py:131
  634.9 92.7 %reduce-scatter.3.cloned.1.call-start = ((), (), s32[]{:S(2)}) async-start(), calls=%async_computation.7 | async-start | bytes 1310720 | tf_op jit(solution)/shard_map/reduce_scatter | solution.py:101
  685.3 35.4 %copy-start = (bf16[128,1024]{1,0:T(8,128)(2,1)S(1)}, bf16[128,1024]{1,0:T(8,128)(2,1)}, u32[]{:S(2)}) copy-start(bf16[128,1024]{1,0:T(8,128)(2,1)} %add_convert_fusion) | copy-start | bytes 786436
Sparse Core Ops, SparseCore 0:
  78.2 18.8 all-gather.4
  98.6 252.4 all-gather.6
  352.7 250.6 all-gather.8
  612.6 39.5 all-gather.10
  654.6 23.7 reduce-scatter.4
  686.6 24.0 reduce-scatter.2
where the time goes:
time: 738 us
  waiting for transfers between devices  554 us (75%)
  blocking collectives  65.8 us (9%)
  matrix products  49.4 us (7%)
  starting transfers between devices  36 us (5%)
  between operations  17.5 us (2%)
  other arithmetic  8.21 us (1%)
    all_gather x1, waiting for transfers between devices, local(): lax.all_gather(w_gate, 'ctx', axis=0, tiled=True)  253 us
    all_gather x1, waiting for transfers between devices, local(): lax.all_gather(w_up, 'ctx', axis=0, tiled=True)  245 us
    ppermute x8, starting transfers between devices, passed_along(): return lax.ppermute(block, axis, route)  35.5 us
    psum x1, blocking collectives, local(): lax.psum((loss_part, count_part), ('ctx', 'head', 'pair'))  31.7 us
    all_to_all x1, blocking collectives, local(): lax.all_to_all(local_part, 'ctx', split_axis=0, concat_axis=1, tiled=True)  28.4 us
    ppermute x8, waiting for transfers between devices, passed_along(): return lax.ppermute(block, axis, route)  21.8 us
    all_gather x1, waiting for transfers between devices, local(): all_hidden = lax.all_gather(hidden, 'ctx', axis=0, tiled=True)  17.2 us
    all_gather x1, waiting for transfers between devices, local(): gathered = lax.all_gather(residual, ('head', 'pair'), axis=1, tiled=True)  16.9 us
  transfers between devices with their start and end apart: 14, of which 12 were waited for; matrix products, arithmetic and copies ran while one was open for 5% of the time, Pallas kernels for 0%

commit v1 on v0

v1 whole, which is shorter than its diff:
```python
import math

import jax
import jax.numpy as jnp
from jax import lax
from jax.sharding import PartitionSpec as P

D = 4096
HEADS = 32
KV_HEADS = 8
HEAD_DIM = 128
TILE = 128


def attend_heads(query_part, key_rows, value_rows, allowed):
    scores = jnp.einsum("thd,sd->hts", query_part, key_rows, preferred_element_type=jnp.float32) * (
        1.0 / math.sqrt(HEAD_DIM)
    )
    masked = jnp.where(allowed[None], scores, -jnp.inf)
    highest = jnp.max(masked, axis=-1, keepdims=True)
    weights = jnp.exp(masked - highest)
    normalized = (weights / jnp.sum(weights, axis=-1, keepdims=True)).astype(jnp.bfloat16)
    return jnp.einsum("hts,sd->thd", normalized, value_rows, preferred_element_type=jnp.float32)


def local(
    student_query,
    teacher_keys,
    teacher_values,
    band_span,
    residual_in,
    norm_gain,
    w_gate,
    w_up,
    w_down,
    teacher_feats,
    keep_tiles,
):
    tok_rows = student_query.shape[0]
    kv_local = teacher_keys.shape[1] // HEAD_DIM
    group_size = HEADS // KV_HEADS
    ctx_index = lax.axis_index("ctx")
    paired = jnp.concatenate([teacher_keys, teacher_values], axis=1)
    all_kv = lax.all_gather(paired, "ctx", axis=0, tiled=True)
    total_rows = all_kv.shape[0]
    key_pos = jnp.arange(total_rows, dtype=jnp.int32)
    query_pos = ctx_index * tok_rows + jnp.arange(tok_rows, dtype=jnp.int32)
    distance = query_pos[:, None] - key_pos[None, :]
    allowed = (distance >= 0) & (distance < band_span[:, None])
    keys_flat = all_kv[:, : kv_local * HEAD_DIM].reshape(total_rows, kv_local, HEAD_DIM)
    values_flat = all_kv[:, kv_local * HEAD_DIM :].reshape(total_rows, kv_local, HEAD_DIM)
    query_heads = student_query.reshape(tok_rows, kv_local, group_size, HEAD_DIM)
    outputs = []
    for kv_head in range(kv_local):
        for first_head in range(0, group_size, 2):
            outputs.append(
                attend_heads(
                    query_heads[:, kv_head, first_head : first_head + 2],
                    keys_flat[:, kv_head],
                    values_flat[:, kv_head],
                    allowed,
                )
            )
    attended = jnp.concatenate(outputs, axis=1).reshape(tok_rows, -1)
    residual = (residual_in.astype(jnp.float32) + attended).astype(jnp.bfloat16)
    resid_own = residual.astype(jnp.float32)
    square_sum = lax.psum(jnp.sum(resid_own * resid_own, axis=1, keepdims=True), ("head", "pair"))
    rms_value = jnp.sqrt(square_sum / D + 1e-05)
    own_cols = residual.shape[1]
    own_start = lax.axis_index(("head", "pair")) * own_cols
    gain_own = lax.dynamic_slice_in_dim(norm_gain, own_start, own_cols, 0)
    scaled = (resid_own * gain_own).astype(jnp.bfloat16)
    wide = lax.all_gather(scaled, ("head", "pair"), axis=1, tiled=True)
    rows = lax.all_to_all(wide, "ctx", split_axis=1, concat_axis=0, tiled=True)
    ff_local = w_gate.shape[1]
    partial = jnp.concatenate(
        [
            jnp.dot(rows, w_gate, preferred_element_type=jnp.float32).astype(jnp.bfloat16),
            jnp.dot(rows, w_up, preferred_element_type=jnp.float32).astype(jnp.bfloat16),
        ],
        axis=1,
    )
    both = lax.psum_scatter(partial, "ctx", scatter_dimension=0, tiled=True).astype(jnp.float32)
    both = both / rms_value
    gate_proj, up_proj = both[:, :ff_local], both[:, ff_local:]
    lifted = jnp.maximum(gate_proj, 0.0)
    squared = lifted * lifted
    act_value = squared * up_proj
    hidden = act_value.astype(jnp.bfloat16)
    tile_count = keep_tiles.shape[1]
    keep_float = keep_tiles.astype(jnp.float32)
    keep_wide = jnp.broadcast_to(keep_float[:, :, None], (tok_rows, tile_count, TILE)).reshape(
        tok_rows, tile_count * TILE
    )
    differ = act_value - teacher_feats.astype(jnp.float32)
    loss_part = jnp.sum(keep_wide * differ * differ)
    count_part = jnp.sum(keep_float) * TILE
    loss_total, count_total = lax.psum((loss_part, count_part), ("ctx", "head", "pair"))
    loss_value = (loss_total / count_total).reshape(1)
    grad_act = keep_wide * differ
    grad_gate = (grad_act * up_proj * 2.0 * lifted).astype(jnp.bfloat16)
    grad_up = (grad_act * squared).astype(jnp.bfloat16)
    all_hidden = lax.all_gather(hidden, "ctx", axis=0, tiled=True)
    all_gate = lax.all_gather(grad_gate, "ctx", axis=0, tiled=True)
    all_up = lax.all_gather(grad_up, "ctx", axis=0, tiled=True)
    contract = (((1,), (1,)), ((), ()))

    def own_sum(part):
        mine = lax.psum_scatter(
            part.astype(jnp.bfloat16), ("head", "pair"), scatter_dimension=1, tiled=True
        )
        byctx = lax.all_to_all(mine, "ctx", split_axis=0, concat_axis=0, tiled=True)
        blocks = lax.axis_size("ctx")
        width = byctx.shape[1]
        byctx = byctx.reshape(blocks, tok_rows, width)
        back = lax.all_to_all(byctx, ("head", "pair"), split_axis=0, concat_axis=2, tiled=True)
        return jnp.swapaxes(back, 0, 1).reshape(tok_rows, own_cols).astype(jnp.float32)

    down_sum = own_sum(jnp.dot(all_hidden, w_down, preferred_element_type=jnp.float32))
    layer_out = (resid_own + down_sum).astype(jnp.bfloat16)
    grad_part = lax.dot_general(all_gate, w_gate, contract, preferred_element_type=jnp.float32)
    grad_part = grad_part + lax.dot_general(
        all_up, w_up, contract, preferred_element_type=jnp.float32
    )
    grad_norm = own_sum(grad_part)
    rms_cubed = rms_value * rms_value * rms_value
    inner_sum = lax.psum(
        jnp.sum(gain_own * grad_norm * resid_own, axis=1, keepdims=True), ("head", "pair")
    )
    grad_resid = gain_own * grad_norm / rms_value - resid_own * inner_sum / (D * rms_cubed)
    return (layer_out, loss_value, grad_resid)


def solution(mesh):
    in_specs = (
        P(("groups", "ctx"), ("head", "pair")),
        P(("groups", "ctx"), ("head", "pair")),
        P(("groups", "ctx"), ("head", "pair")),
        P(("groups", "ctx")),
        P(("groups", "ctx"), ("head", "pair")),
        P(),
        P("ctx", ("head", "pair")),
        P("ctx", ("head", "pair")),
        P(("head", "pair"), "ctx"),
        P(("groups", "ctx"), ("head", "pair")),
        P(("groups", "ctx"), ("head", "pair")),
    )
    out_specs = (
        P(("groups", "ctx"), ("head", "pair")),
        P("groups"),
        P(("groups", "ctx"), ("head", "pair")),
    )
    return jax.shard_map(local, mesh=mesh, in_specs=in_specs, out_specs=out_specs, check_vma=False)
```

time: 738 us -> 414 us (0.56)
  waiting for transfers between devices: 554 us -> 235 us
  blocking collectives: 65.8 us -> 107 us
  starting transfers between devices: 36 us -> 11.9 us
  matrix products: 49.4 us -> 26.1 us
    all_gather x3, waiting for transfers between devices: 514 us -> 95.3 us  [the longest x1 40.7 us: local(): all_gate = lax.all_gather(grad_gate, 'ctx', axis=0, tiled=True)]
    reduce_scatter x2 -> x3, waiting for transfers between devices: 0.02 us -> 103 us  [the longest x1 59.7 us: local(): lax.psum_scatter(partial, 'ctx', scatter_dimension=0, tiled=True)]
    ppermute x8 -> x0, starting transfers between devices: 35.5 us -> none  [passed_along(): return lax.ppermute(block, axis, route)]
    ppermute x8 -> x0, waiting for transfers between devices: 21.8 us -> none  [passed_along(): return lax.ppermute(block, axis, route)]
    dot_general x4 -> x8, matrix products: 39.1 us -> 17.7 us  [the longest x1 5.65 us: local(): lax.dot_general(all_up, w_up, contract, preferred_element_type=jnp.float32)]
    all_gather x1, waiting for transfers between devices: 17.2 us -> 35.8 us  [local(): all_hidden = lax.all_gather(hidden, 'ctx', axis=0, tiled=True)]
    all_gather x0 -> x1, blocking collectives: none -> 16.7 us  [local(): all_kv = lax.all_gather(paired, 'ctx', axis=0, tiled=True)]
    all_to_all x1 -> x2, blocking collectives: 28.4 us -> 44.3 us  [the longest x1 30.7 us: local(): rows = lax.all_to_all(wide, 'ctx', split_axis=1, concat_axis=0, tiled=True)]
  transfers between devices with their start and end apart: 14 -> 10, of which waited for: 12 -> 7; matrix products, arithmetic and copies ran while one was open for 5% -> 4% of each run, Pallas kernels for 0% -> 0%
where the time goes in v1:
time: 414 us
  waiting for transfers between devices  235 us (57%)
  blocking collectives  107 us (26%)
  matrix products  26.1 us (6%)
  between operations  17.6 us (4%)
  starting transfers between devices  11.9 us (3%)
  other arithmetic  8.81 us (2%)
  local copies, waits for them, and re-layouts  6.73 us (2%)
    reduce_scatter x1, waiting for transfers between devices, local(): lax.psum_scatter(partial, 'ctx', scatter_dimension=0, tiled=True)  59.7 us
    reduce_scatter x2, waiting for transfers between devices, own_sum(): lax.psum_scatter(part.astype(jnp.bfloat16), ('head', 'pair'), scatter_dim...  43.5 us
    all_gather x1, waiting for transfers between devices, local(): all_gate = lax.all_gather(grad_gate, 'ctx', axis=0, tiled=True)  40.7 us
    all_gather x1, waiting for transfers between devices, local(): all_up = lax.all_gather(grad_up, 'ctx', axis=0, tiled=True)  37.6 us
    all_gather x1, waiting for transfers between devices, local(): all_hidden = lax.all_gather(hidden, 'ctx', axis=0, tiled=True)  35.8 us
    psum x1, blocking collectives, local(): lax.psum((loss_part, count_part), ('ctx', 'head', 'pair'))  32.8 us
    all_to_all x1, blocking collectives, local(): rows = lax.all_to_all(wide, 'ctx', split_axis=1, concat_axis=0, tiled=True)  30.7 us
    all_gather x1, waiting for transfers between devices, local(): wide = lax.all_gather(scaled, ('head', 'pair'), axis=1, tiled=True)  16.9 us
  transfers between devices with their start and end apart: 10, of which 7 were waited for; matrix products, arithmetic and copies ran while one was open for 4% of the time, Pallas kernels for 0%

profile of v1, /device:TPU:0, one launch (start us, length us, event | category | flops | bytes accessed | tf_op | source)
XLA Modules:
  0.0 413.6 jit_solution(905727227815963759)
XLA Ops:
  7.2 1.0 copy.41
  8.2 1.0 copy.42
  9.2 16.7 %all_gather.15 = bf16[512,512]{0,1:T(8,128)(2,1)S(1)} all-gather(bf16[128,512]{0,1:T(8,128)(2,1)S(1)} %pad_maximum_fusion.2), channel_id=1, replica_groups=mesh['groups'=2,'ctx'=4,'head'=2,'pair'=2] {'ctx'}, dimensions={0}, use_global_device_ids=true | all-gather | bytes 655360 | tf_op jit(solution)/shard_map/all_gather | solution.py:44
  26.2 0.3 fusion.19
  26.4 0.4 fusion.51
  26.8 0.2 fusion.17
  27.1 0.4 fusion.50
  27.7 0.4 fusion.49
  28.1 0.3 fusion.13
  28.4 0.4 fusion.48
  29.0 0.3 convolution_bitcast_fusion.3
  29.3 0.3 convolution_bitcast_fusion.2
  29.6 0.3 convolution_bitcast_fusion.1
  29.9 0.3 convolution_bitcast_fusion
  30.4 0.7 dynamic_slice.3
  31.1 0.9 fusion.21
  32.1 16.9 %all-gather.5.cloned.1.call-done = bf16[128,4096]{0,1:T(8,128)(2,1)} async-done(((bf16[128,1024]{0,1:T(8,128)(2,1)}), bf16[128,4096]{0,1:T(8,128)(2,1)}) %all-gather.5.cloned.1.call-update) | async-done | bytes 1048592 | tf_op jit(solution)/shard_map/all_gather | solution.py:73
  49.0 30.7 %all_to_all.55 = bf16[128,4,1024]{0,2,1:T(8,128)(2,1)S(1)} all-to-all(bf16[128,4,1024]{0,2,1:T(8,128)(2,1)} %bitcast.182), channel_id=1, replica_groups=mesh['groups'=2,'ctx'=4,'head'=2,'pair'=2] {'ctx'}, dimensions={1} | all-to-all | bytes 2097152 | tf_op jit(solution)/shard_map/all_to_all | solution.py:74
  79.8 0.5 copy.54
  80.3 4.3 %convolution_convert_fusion = bf16[512,1792]{1,0:T(8,128)(2,1)S(1)} fusion(bf16[512,1024]{1,0:T(8,128)(2,1)S(1)} %bitcast.183, bf16[1024,1792]{1,0:T(8,128)(2,1)} %param.18), kind=kOutput, calls=%fused_computation.5 | convolution fusion | flops 1879965696 | bytes 6553600 | tf_op jit(solution)/shard_map/dot_general | solution.py:79
  84.6 2.1 convolution_convert_fusion.1
  86.7 2.1 pad_maximum_fusion
  88.8 0.6 copy-done.3
  89.5 0.3 copy.56
  89.8 5.9 %psum.28 = f32[128,1]{0,1:T(1,128)S(1)} all-reduce(f32[128,1]{0,1:T(1,128)S(1)} %bitcast.191), channel_id=1, replica_groups=mesh['groups'=2,'ctx'=4,'head'=2,'pair'=2] {'head','pair'}, use_global_device_ids=true, to_apply=%region_10.11 | all-reduce | flops 128 | bytes 1024 | tf_op jit(solution)/shard_map/psum | solution.py:67
  95.8 59.7 %reduce-scatter.4.cloned.1.call-done = bf16[128,3584]{1,0:T(8,128)(2,1)} async-done(((bf16[512,3584]{1,0:T(8,128)(2,1)}), bf16[128,3584]{1,0:T(8,128)(2,1)}) %reduce-scatter.4.cloned.1.call-update) | async-done | bytes 917520 | tf_op jit(solution)/shard_map/reduce_scatter | solution.py:83
  155.5 1.4 convert_divide_fusion
  156.9 1.1 multiply_convert_fusion
  158.0 1.9 multiply_convert_fusion.1
  160.0 0.5 all-gather.11.cloned.1.call-update
  160.6 0.5 all-gather.7.cloned.1.call-update
  161.1 40.7 %all-gather.9.cloned.1.call-done = bf16[512,1792]{1,0:T(8,128)(2,1)} async-done(((bf16[128,1792]{1,0:T(8,128)(2,1)}), bf16[512,1792]{1,0:T(8,128)(2,1)}) %all-gather.9.cloned.1.call-update) | async-done | bytes 1835024 | tf_op jit(solution)/shard_map/all_gather | solution.py:104
  201.9 4.7 %fusion.52 = f32[512,1024]{1,0:T(8,128)S(1)} fusion(bf16[512,1792]{1,0:T(8,128)(2,1)} %all-gather.9.cloned.1.call-done, bf16[1024,1792]{1,0:T(8,128)(2,1)} %param.17), kind=kOutput, calls=%fused_computation.99 | convolution fusion | flops 1879048192 | bytes 7602176 | tf_op jit(solution)/shard_map/dot_general | solution.py:121
  206.5 37.6 %all-gather.11.cloned.1.call-done = bf16[512,1792]{1,0:T(8,128)(2,1)} async-done(((bf16[128,1792]{1,0:T(8,128)(2,1)}), bf16[512,1792]{1,0:T(8,128)(2,1)}) %all-gather.11.cloned.1.call-update) | async-done | bytes 1835024 | tf_op jit(solution)/shard_map/all_gather | solution.py:105
  244.2 5.7 %add_convert_fusion = bf16[512,1024]{1,0:T(8,128)(2,1)} fusion(f32[512,1024]{1,0:T(8,128)S(1)} %fusion.52, bf16[512,1792]{1,0:T(8,128)(2,1)} %all-gather.11.cloned.1.call-done, bf16[1024,1792]{1,0:T(8,128)(2,1)} %param.18), kind=kOutput, calls=%fused_computation.7 | convolution fusion | flops 1880096768 | bytes 8650752 | tf_op jit(solution)/shard_map/dot_general | solution.py:122
  250.1 35.8 %all-gather.7.cloned.1.call-done = bf16[512,1792]{1,0:T(8,128)(2,1)} async-done(((bf16[128,1792]{1,0:T(8,128)(2,1)}), bf16[512,1792]{1,0:T(8,128)(2,1)}) %all-gather.7.cloned.1.call-update) | async-done | bytes 1835024 | tf_op jit(solution)/shard_map/all_gather | solution.py:103
  285.9 5.6 %convolution_convert_fusion.2 = bf16[512,1024]{1,0:T(8,128)(2,1)} fusion(bf16[512,1792]{1,0:T(8,128)(2,1)} %all-gather.7.cloned.1.call-done, bf16[1792,1024]{1,0:T(8,128)(2,1)} %param.19), kind=kOutput, calls=%fused_computation.9 | convolution fusion | flops 1879572480 | bytes 6553600 | tf_op jit(solution)/shard_map/dot_general | solution.py:119
  291.5 20.5 %reduce-scatter.8.cloned.1.call-done = bf16[512,256]{1,0:T(8,128)(2,1)} async-done(((bf16[512,1024]{1,0:T(8,128)(2,1)}), bf16[512,256]{1,0:T(8,128)(2,1)}) %reduce-scatter.8.cloned.1.call-update) | async-done | bytes 262160 | tf_op jit(solution)/shard_map/reduce_scatter | solution.py:109
  312.1 4.6 %all-to-all-start.3 = ((bf16[4,128,256]{2,1,0:T(8,128)(2,1)}), bf16[4,128,256]{2,1,0:T(8,128)(2,1)}, u32[]{:S(2)}, u32[]{:S(2)}) async-start(bf16[4,128,256]{2,1,0:T(8,128)(2,1)} %bitcast.185), calls=%async_computation.6 | async-start | bytes 524288 | tf_op jit(solution)/shard_map/all_to_all | solution.py:112
  316.6 23.0 %reduce-scatter.6.cloned.1.call-done = bf16[512,256]{1,0:T(8,128)(2,1)} async-done(((bf16[512,1024]{1,0:T(8,128)(2,1)}), bf16[512,256]{1,0:T(8,128)(2,1)}) %reduce-scatter.6.cloned.1.call-update) | async-done | bytes 262160 | tf_op jit(solution)/shard_map/reduce_scatter | solution.py:109
  339.7 13.6 %all_to_all.56 = bf16[4,128,256]{2,1,0:T(8,128)(2,1)} all-to-all(bf16[4,128,256]{2,1,0:T(8,128)(2,1)} %bitcast.186), channel_id=1, replica_groups=mesh['groups'=2,'ctx'=4,'head'=2,'pair'=2] {'ctx'}, dimensions={0} | all-to-all | bytes 524288 | tf_op jit(solution)/shard_map/all_to_all | solution.py:112
  353.2 3.4 all-to-all-start.4
  356.6 0.6 convert_reduce_fusion
  357.9 32.8 %all-reduce = (f32[]{:T(128)}, f32[]{:T(128)}) all-reduce(f32[]{:T(128)} %get-tuple-element.13, f32[]{:T(128)S(6)} %mul.125), channel_id=1, replica_groups=mesh['groups'=2,'ctx'=4,'head'=2,'pair'=2] {'ctx','head','pair'}, use_global_device_ids=true, to_apply=%region_13.14 | all-reduce | flops 2 | bytes 16 | tf_op jit(solution)/shard_map/psum | solution.py:98
  392.0 3.4 all-to-all-start.2
  395.9 7.4 %psum.31 = f32[128]{0:T(128)S(1)} all-reduce(f32[128]{0:T(128)S(1)} %fusion.24), channel_id=1, replica_groups=mesh['groups'=2,'ctx'=4,'head'=2,'pair'=2] {'head','pair'}, use_global_device_ids=true, to_apply=%region_18.19 | all-reduce | flops 128 | bytes 1024 | tf_op jit(solution)/shard_map/psum | solution.py:127
  403.8 1.0 copy.59
  404.7 0.9 copy.58
  (44 shorter events, 2.5 us)
Async XLA Ops:
  7.2 18.7 %copy-start.1 = (bf16[128,1024]{1,0:T(8,128)(2,1)S(1)}, bf16[128,1024]{1,0:T(8,128)(2,1)}, u32[]{:S(2)}) copy-start(bf16[128,1024]{1,0:T(8,128)(2,1)} %param.11) | copy-start | bytes 786436
  7.2 18.9 %copy-start.4 = (s32[128]{0:T(128)S(1)}, s32[128]{0:T(128)}, u32[]{:S(2)}) copy-start(s32[128]{0:T(128)} %param.14) | copy-start | bytes 1540
  7.2 41.8 %all-gather.5.cloned.1.call-start = ((), (), s32[]{:S(2)}) async-start(), calls=%async_computation.8 | async-start | bytes 1310720 | tf_op jit(solution)/shard_map/all_gather | solution.py:73
  27.5 1.3 copy-start.2
  32.1 123.4 %reduce-scatter.4.cloned.1.call-start = ((), (), s32[]{:S(2)}) async-start(), calls=%async_computation.9 | async-start | bytes 4587520 | tf_op jit(solution)/shard_map/reduce_scatter | solution.py:83
  80.3 4.3 %copy-start.5 = (bf16[1024,1792]{1,0:T(8,128)(2,1)S(1)}, bf16[1024,1792]{1,0:T(8,128)(2,1)}, u32[]{:S(2)}) copy-start(bf16[1024,1792]{1,0:T(8,128)(2,1)} %param.17) | copy-start | bytes 11010052
  88.7 0.7 copy-start.3
  88.8 113.1 %all-gather.9.cloned.1.call-start = ((), (), s32[]{:S(2)}) async-start(), calls=%async_computation.12 | async-start | bytes 2293760 | tf_op jit(solution)/shard_map/all_gather | solution.py:104
  89.5 67.4 %copy-start = (bf16[128,1792]{1,0:T(8,128)(2,1)S(1)}, bf16[128,1792]{1,0:T(8,128)(2,1)}, u32[]{:S(2)}) copy-start(bf16[128,1792]{1,0:T(8,128)(2,1)} %param.20) | copy-start | bytes 1376260
  159.9 84.2 %all-gather.11.cloned.1.call-start = ((), (), s32[]{:S(2)}) async-start(), calls=%async_computation.13 | async-start | bytes 2293760 | tf_op jit(solution)/shard_map/all_gather | solution.py:105
  160.5 125.4 %all-gather.7.cloned.1.call-start = ((), (), s32[]{:S(2)}) async-start(), calls=%async_computation.10 | async-start | bytes 2293760 | tf_op jit(solution)/shard_map/all_gather | solution.py:103
  161.1 151.0 %reduce-scatter.8.cloned.1.call-start = ((), (), s32[]{:S(2)}) async-start(), calls=%async_computation.14 | async-start | bytes 1310720 | tf_op jit(solution)/shard_map/reduce_scatter | solution.py:109
  249.8 89.8 %reduce-scatter.6.cloned.1.call-start = ((), (), s32[]{:S(2)}) async-start(), calls=%async_computation.11 | async-start | bytes 1310720 | tf_op jit(solution)/shard_map/reduce_scatter | solution.py:109
  312.1 27.6 %all-to-all-start.3 = ((bf16[4,128,256]{2,1,0:T(8,128)(2,1)}), bf16[4,128,256]{2,1,0:T(8,128)(2,1)}, u32[]{:S(2)}, u32[]{:S(2)}) async-start(bf16[4,128,256]{2,1,0:T(8,128)(2,1)} %bitcast.185), calls=%async_computation.6 | async-start | bytes 524288 | tf_op jit(solution)/shard_map/all_to_all | solution.py:112
  353.2 38.8 %all-to-all-start.4 = ((bf16[4,128,256]{2,1,0:T(8,128)(2,1)}), bf16[4,128,256]{2,1,0:T(8,128)(2,1)S(1)}, u32[]{:S(2)}, u32[]{:S(2)}) async-start(bf16[4,128,256]{2,1,0:T(8,128)(2,1)} %all-to-all-done.3), calls=%async_computation.7 | async-start | bytes 524288 | tf_op jit(solution)/shard_map/all_to_all | solution.py:116
  392.0 11.3 %all-to-all-start.2 = ((bf16[4,128,256]{2,1,0:T(8,128)(2,1)}), bf16[4,128,256]{2,1,0:T(8,128)(2,1)S(1)}, u32[]{:S(2)}, u32[]{:S(2)}) async-start(bf16[4,128,256]{2,1,0:T(8,128)(2,1)} %all_to_all.56), calls=%async_computation.4 | async-start | bytes 524288 | tf_op jit(solution)/shard_map/all_to_all | solution.py:116
Sparse Core Ops, SparseCore 0:
  32.2 16.8 all-gather.4
  88.9 66.5 reduce-scatter.3
  160.0 41.7 all-gather.8
  203.9 40.2 all-gather.10
  245.6 40.2 all-gather.6
  288.2 23.7 reduce-scatter.7
  314.7 24.8 reduce-scatter.5

commit v2 on v1

v2 whole, which is shorter than its diff:
```python
import functools
import math

import jax
import jax.numpy as jnp
from jax import lax
from jax.experimental import pallas as pl
from jax.experimental.pallas import tpu as pltpu
from jax.sharding import PartitionSpec as P

HEAD_DIM = 128
TILE = 128
CHUNKS = 7
MESH = pl.DeviceIdType.MESH
F32 = jnp.float32
BF16 = jnp.bfloat16


def layer_kernel(
    nc, nhead, npair, chunks,
    q_ref, k_ref, v_ref, span_ref, res_ref, gain_ref, wg_hbm, wu_hbm, wd_hbm, feats_ref, keep_ref,
    out_ref, loss_ref, grad_ref,
    wg, wu, wd, kbuf, vbuf, resid, squares, nbuf, xall, tmp, part, fromleft, fromright, own,
    gathered, acc_down, acc_grad, keep_wide, sums, pair_in, head_in, final, inner, loss_head,
    loss_ctx, loss_acc,
    w_sem, kv_send, kv_recv, sq_send, sq_recv, n_send, n_recv, x_send, x_recv, rs_send, right_recv,
    left_recv, ag_send, ag_recv, p_send, p_recv, h_send, h_recv, f_send, f_recv, in_send, in_recv,
    lh_send, lh_recv, lc_send, lc_recv,
):
    nh = nhead * npair
    nb = nc // nh
    rows = q_ref.shape[0]
    sub = rows // nh
    dc = wg.shape[0]
    width = nc * dc
    ff = wg.shape[1]
    cw = ff // chunks
    c = lax.axis_index("ctx")
    my_head = lax.axis_index("head")
    my_pair = lax.axis_index("pair")
    h = my_head * npair + my_pair

    def remote(src, dst, send, recv, to_c, to_h):
        return pltpu.make_async_remote_copy(
            src_ref=src, dst_ref=dst, send_sem=send, recv_sem=recv,
            device_id={"ctx": to_c, "head": to_h // npair, "pair": to_h % npair},
            device_id_type=MESH,
        )

    weight_copies = [
        pltpu.make_async_copy(a, b, w_sem.at[i])
        for i, (a, b) in enumerate(((wg_hbm, wg), (wu_hbm, wu), (wd_hbm, wd)))
    ]
    for copy in weight_copies:
        copy.start()

    barrier = pltpu.get_barrier_semaphore()

    def greet(i, carry):
        to_c, to_h = i // nh, i % nh

        @pl.when((to_c != c) | (to_h != h))
        def _():
            pl.semaphore_signal(
                barrier, inc=1,
                device_id={"ctx": to_c, "head": to_h // npair, "pair": to_h % npair},
                device_id_type=MESH,
            )

        return carry

    lax.fori_loop(0, nc * nh, greet, 0)
    pl.semaphore_wait(barrier, nc * nh - 1)

    def kv_copies(block, to_c):
        return (
            remote(kbuf.at[block], kbuf.at[block], kv_send.at[0, to_c], kv_recv.at[0, block], to_c, h),
            remote(vbuf.at[block], vbuf.at[block], kv_send.at[1, to_c], kv_recv.at[1, block], to_c, h),
        )

    kbuf[c] = k_ref[...]
    vbuf[c] = v_ref[...]
    for other in range(nc):
        @pl.when(other > c)
        def _(other=other):
            for copy in kv_copies(c, other):
                copy.start()
            kbuf[other] = jnp.zeros_like(k_ref)
            vbuf[other] = jnp.zeros_like(v_ref)
    tile_count = keep_ref.shape[1]
    for t in range(tile_count):
        keep_wide[:, t * TILE : (t + 1) * TILE] = jnp.broadcast_to(
            keep_ref[:, t : t + 1].astype(F32), (rows, TILE)
        ).astype(BF16)
    for other in range(nc):
        @pl.when(other < c)
        def _(other=other):
            for copy in kv_copies(other, c):
                copy.wait_recv()

    span = nc * rows
    key_pos = lax.broadcasted_iota(jnp.int32, (rows, span), 1)
    query_pos = c * rows + lax.broadcasted_iota(jnp.int32, (rows, span), 0)
    distance = query_pos - key_pos
    allowed = (distance >= 0) & (distance < span_ref[...])
    kv_heads = k_ref.shape[1] // HEAD_DIM
    heads = q_ref.shape[1] // HEAD_DIM
    per = heads // kv_heads
    for kv in range(kv_heads):
        kcols = slice(kv * HEAD_DIM, (kv + 1) * HEAD_DIM)
        keys = kbuf[:, :, kcols].reshape(span, HEAD_DIM)
        values = vbuf[:, :, kcols].reshape(span, HEAD_DIM)
        for a in range(kv * per, (kv + 1) * per):
            cols = slice(a * HEAD_DIM, (a + 1) * HEAD_DIM)
            scores = lax.dot_general(
                q_ref[:, cols], keys, (((1,), (1,)), ((), ())), preferred_element_type=F32
            ) * (1.0 / math.sqrt(HEAD_DIM))
            masked = jnp.where(allowed, scores, -jnp.inf)
            weights = jnp.exp(masked - jnp.max(masked, axis=-1, keepdims=True))
            probs = (weights / jnp.sum(weights, axis=-1, keepdims=True)).astype(BF16)
            attended = jnp.dot(probs, values, preferred_element_type=F32)
            resid[:, cols] = (res_ref[:, cols].astype(F32) + attended).astype(BF16)

    def peers(body):
        for other in range(nh):
            @pl.when(other != h)
            def _(other=other):
                body(other)

    def exchange(buf, send, recv):
        peers(lambda o: remote(buf.at[h], buf.at[h], send.at[o], recv.at[h], c, o).start())
        peers(lambda o: remote(buf.at[o], buf.at[o], send.at[o], recv.at[o], c, o).wait_recv())
        total = buf[0]
        for other in range(1, nh):
            total = total + buf[other]
        return total

    def exchange_end(buf, send, recv):
        peers(lambda o: remote(buf.at[h], buf.at[h], send.at[o], recv.at[h], c, o).wait_send())

    resid_own = resid[...].astype(F32)
    squares[h] = jnp.broadcast_to(
        jnp.sum(resid_own * resid_own, axis=1, keepdims=True), (rows, TILE)
    )
    rms = jnp.sqrt(exchange(squares, sq_send, sq_recv)[:, :1] / width + 1e-05)

    normed = (resid[...].astype(F32) / rms * gain_ref[...]).astype(BF16)
    for b in range(nb):
        nbuf[b] = normed[:, b * dc : (b + 1) * dc].reshape(nh, sub, dc)

    def hop_one(b, other):
        to_c = h * nb + b
        return remote(
            nbuf.at[b, other], xall.at[c, other], n_send.at[b, other], n_recv.at[c], to_c, other
        )

    for b in range(nb):
        for other in range(nh):
            mine = (h * nb + b == c) & (other == h)

            @pl.when(jnp.logical_not(mine))
            def _(b=b, other=other):
                hop_one(b, other).start()

            @pl.when(mine)
            def _(b=b, other=other):
                xall[c, other] = nbuf[b, other]

    source_h = c // nb
    for other in range(nc):
        @pl.when((other != c) | (source_h != h))
        def _(other=other):
            remote(
                xall.at[other, h], xall.at[other, h], n_send.at[0, 0], n_recv.at[other],
                other, source_h,
            ).wait_recv()

    def hop_two(row_h, to_h):
        return remote(
            xall.at[:, row_h], xall.at[:, row_h], x_send.at[to_h], x_recv.at[row_h], c, to_h
        )

    peers(lambda o: hop_two(h, o).start())
    for copy in weight_copies:
        copy.wait()
    peers(lambda o: hop_two(o, o).wait_recv())

    def cols_of(j):
        return pl.ds(pl.multiple_of(j * cw, cw), cw)

    def rs_copy(j, dest, to_c, buf, recv):
        return remote(
            part.at[j, dest], buf.at[j, dest], rs_send.at[j, dest], recv.at[j, dest], to_c, h
        )

    def go_right(j, dest):
        return rs_copy(j, dest, lax.rem(c + 1, nc), fromleft, right_recv)

    def go_left(j, dest):
        return rs_copy(j, dest, lax.rem(c + nc - 1, nc), fromright, left_recv)

    def multiply(j, carry):
        def block(i, inner_carry):
            x = xall[i].reshape(rows, dc)
            tmp[i, :, 0:cw] = jnp.dot(x, wg[:, cols_of(j)], preferred_element_type=F32)
            tmp[i, :, cw : 2 * cw] = jnp.dot(x, wu[:, cols_of(j)], preferred_element_type=F32)
            part[j, i] = tmp[i].astype(BF16)
            return inner_carry

        lax.fori_loop(0, nc, block, 0)
        own[j] = tmp[c]
        for dest in range(nc - 1, 0, -1):
            @pl.when(c == 0)
            def _(dest=dest):
                go_right(j, dest).start()
        for dest in range(nc - 1):
            @pl.when(c == nc - 1)
            def _(dest=dest):
                go_left(j, dest).start()
        return carry

    lax.fori_loop(0, chunks, multiply, 0)

    def reduce_on(j):
        for far in range(nc - 1):
            dest = nc - 1 - far

            @pl.when((c > 0) & (c < dest))
            def _(dest=dest):
                go_right(j, dest).wait_recv()
                part[j, dest] = (part[j, dest].astype(F32) + fromleft[j, dest].astype(F32)).astype(BF16)
                go_right(j, dest).start()

            @pl.when((c < nc - 1) & (c > far))
            def _(dest=far):
                go_left(j, dest).wait_recv()
                part[j, dest] = (part[j, dest].astype(F32) + fromright[j, dest].astype(F32)).astype(BF16)
                go_left(j, dest).start()

    def gather_copy(j, block, direction):
        to_c = lax.rem(c + 1, nc) if direction == 0 else lax.rem(c + nc - 1, nc)
        return remote(
            gathered.at[j, block], gathered.at[j, block], ag_send.at[direction, j, block],
            ag_recv.at[j, block], to_c, h,
        )

    loss_acc[...] = jnp.zeros_like(loss_acc)

    def features(j):
        @pl.when(c > 0)
        def _():
            go_right(j, c).wait_recv()
            own[j] = own[j] + fromleft[j, c].astype(F32)

        @pl.when(c < nc - 1)
        def _():
            go_left(j, c).wait_recv()
            own[j] = own[j] + fromright[j, c].astype(F32)

        gate = own[j, :, 0:cw]
        up = own[j, :, cw : 2 * cw]
        lifted = jnp.maximum(gate, 0.0)
        squared = lifted * lifted
        act = squared * up
        keep = keep_wide[:, cols_of(j)].astype(F32)
        differ = act - feats_ref[:, cols_of(j)].astype(F32)
        grad_act = keep * differ
        loss_acc[...] += grad_act * differ
        gathered[j, c, :, 0:cw] = act.astype(BF16)
        gathered[j, c, :, cw : 2 * cw] = (grad_act * up * 2.0 * lifted).astype(BF16)
        gathered[j, c, :, 2 * cw : 3 * cw] = (grad_act * squared).astype(BF16)

        @pl.when(c < nc - 1)
        def _():
            gather_copy(j, c, 0).start()

        @pl.when(c > 0)
        def _():
            gather_copy(j, c, 1).start()

    def forward(j):
        for far in range(1, nc):
            @pl.when(c >= far)
            def _(far=far):
                block = lax.rem(c - far + nc, nc)
                gather_copy(j, block, 0).wait_recv()

                @pl.when(c < nc - 1)
                def _():
                    gather_copy(j, block, 0).start()

            @pl.when(c + far < nc)
            def _(far=far):
                block = lax.rem(c + far, nc)
                gather_copy(j, block, 1).wait_recv()

                @pl.when(c > 0)
                def _():
                    gather_copy(j, block, 1).start()

    contract = (((1,), (1,)), ((), ()))
    acc_down[...] = jnp.zeros_like(acc_down)
    acc_grad[...] = jnp.zeros_like(acc_grad)

    def accumulate(j):
        def block(i, carry):
            hidden = gathered[j, i, :, 0:cw]
            grad_gate = gathered[j, i, :, cw : 2 * cw]
            grad_up = gathered[j, i, :, 2 * cw : 3 * cw]
            acc_down[i] += jnp.dot(hidden, wd[cols_of(j), :], preferred_element_type=F32)
            acc_grad[i] += lax.dot_general(
                grad_gate, wg[:, cols_of(j)], contract, preferred_element_type=F32
            ) + lax.dot_general(grad_up, wu[:, cols_of(j)], contract, preferred_element_type=F32)
            return carry

        lax.fori_loop(0, nc, block, 0)

    def step(i, carry):
        @pl.when(i < chunks)
        def _():
            reduce_on(i)

        @pl.when((i >= 1) & (i < chunks + 1))
        def _():
            features(i - 1)

        @pl.when(i >= 2)
        def _():
            forward(i - 2)
            accumulate(i - 2)

        return carry

    lax.fori_loop(0, chunks + 2, step, 0)

    loss_part = jnp.sum(jnp.sum(loss_acc[...], axis=1, keepdims=True), axis=0, keepdims=True)
    count_part = jnp.sum(
        jnp.sum(keep_ref[...].astype(F32), axis=1, keepdims=True), axis=0, keepdims=True
    ) * TILE
    line = lax.broadcasted_iota(jnp.int32, (8, TILE), 0)
    loss_head[h] = jnp.where(line == 0, loss_part, count_part)
    peers(lambda o: remote(loss_head.at[h], loss_head.at[h], lh_send.at[o], lh_recv.at[h], c, o).start())

    for p in range(npair):
        for g in range(nhead):
            o = g * npair + p
            for i in range(nc):
                sums[p, g, i, 0] = acc_down[i, o * sub : (o + 1) * sub].astype(BF16)
                sums[p, g, i, 1] = acc_grad[i, o * sub : (o + 1) * sub].astype(BF16)

    def pair_copy(p):
        return remote(
            sums.at[p], pair_in.at[my_pair], p_send.at[p], p_recv.at[my_pair], c, my_head * npair + p
        )

    def pair_wait(p):
        return remote(
            sums.at[p], pair_in.at[p], p_send.at[p], p_recv.at[p], c, my_head * npair + p
        )

    for p in range(npair):
        @pl.when(p != my_pair)
        def _(p=p):
            pair_copy(p).start()
    for p in range(npair):
        @pl.when(p != my_pair)
        def _(p=p):
            pair_wait(p).wait_recv()

            def add(i, carry):
                g, k = i // nc, i % nc
                sums[my_pair, g, k] = (
                    sums[my_pair, g, k].astype(F32) + pair_in[p, g, k].astype(F32)
                ).astype(BF16)
                return carry

            lax.fori_loop(0, nhead * nc, add, 0)

    def head_copy(g):
        return remote(
            sums.at[my_pair, g], head_in.at[my_head], h_send.at[g], h_recv.at[my_head],
            c, g * npair + my_pair,
        )

    def head_wait(g):
        return remote(
            sums.at[my_pair, g], head_in.at[g], h_send.at[g], h_recv.at[g],
            c, g * npair + my_pair,
        )

    for g in range(nhead):
        @pl.when(g != my_head)
        def _(g=g):
            head_copy(g).start()

    peers(lambda o: remote(loss_head.at[o], loss_head.at[o], lh_send.at[o], lh_recv.at[o], c, o).wait_recv())
    head_total = loss_head[0]
    for other in range(1, nh):
        head_total = head_total + loss_head[other]
    loss_ctx[c] = head_total

    def loss_copy(block, to_c):
        return remote(
            loss_ctx.at[block], loss_ctx.at[block], lc_send.at[to_c], lc_recv.at[block], to_c, h
        )

    for other in range(nc):
        @pl.when(other != c)
        def _(other=other):
            loss_copy(c, other).start()

    for g in range(nhead):
        @pl.when(g != my_head)
        def _(g=g):
            head_wait(g).wait_recv()

            def add(k, carry):
                sums[my_pair, my_head, k] = (
                    sums[my_pair, my_head, k].astype(F32) + head_in[g, k].astype(F32)
                ).astype(BF16)
                return carry

            lax.fori_loop(0, nc, add, 0)

    to_h = c // nb
    slot = lax.rem(c, nb) if nb > 1 else 0

    def final_copy(block):
        return remote(
            sums.at[my_pair, my_head, block], final.at[slot, h], f_send.at[block],
            f_recv.at[slot, h], block, to_h,
        )

    for block in range(nc):
        mine = (block == c) & (to_h == h)

        @pl.when(jnp.logical_not(mine))
        def _(block=block):
            final_copy(block).start()

        @pl.when(mine)
        def _(block=block):
            final[slot, h] = sums[my_pair, my_head, block]

    for b in range(nb):
        for other in range(nh):
            from_c = h * nb + b

            @pl.when((from_c != c) | (other != h))
            def _(b=b, other=other, from_c=from_c):
                remote(
                    final.at[b, other], final.at[b, other], f_send.at[0], f_recv.at[b, other],
                    from_c, other,
                ).wait_recv()

    inner_part = jnp.zeros((rows, 1), F32)
    for b in range(nb):
        cols = slice(b * dc, (b + 1) * dc)
        down = final[b, :, 0].reshape(rows, dc).astype(F32)
        out_ref[:, cols] = (resid[:, cols].astype(F32) + down).astype(BF16)
        grad_norm = final[b, :, 1].reshape(rows, dc).astype(F32)
        inner_part += jnp.sum(
            gain_ref[:, cols] * grad_norm * resid[:, cols].astype(F32), axis=1, keepdims=True
        )
    inner[h] = jnp.broadcast_to(inner_part, (rows, TILE))
    inner_sum = exchange(inner, in_send, in_recv)[:, :1]
    rms = jnp.sqrt(
        functools.reduce(lambda a, b: a + b, [squares[o] for o in range(nh)])[:, :1] / width + 1e-05
    )
    scale = inner_sum / (width * (rms * rms * rms))
    for b in range(nb):
        cols = slice(b * dc, (b + 1) * dc)
        grad_norm = final[b, :, 1].reshape(rows, dc).astype(F32)
        grad_ref[:, cols] = (
            gain_ref[:, cols] * grad_norm / rms - resid[:, cols].astype(F32) * scale
        )

    for other in range(nc):
        @pl.when(other != c)
        def _(other=other):
            loss_copy(other, other).wait_recv()
    total = loss_ctx[0]
    for other in range(1, nc):
        total = total + loss_ctx[other]
    loss_ref[...] = jnp.broadcast_to(total[0:1] / total[1:2], (8, TILE))

    for other in range(nc):
        @pl.when(other > c)
        def _(other=other):
            for copy in kv_copies(c, other):
                copy.wait_send()

        @pl.when(other != c)
        def _(other=other):
            loss_copy(c, other).wait_send()

    exchange_end(squares, sq_send, sq_recv)
    exchange_end(inner, in_send, in_recv)
    for b in range(nb):
        for other in range(nh):
            @pl.when((h * nb + b != c) | (other != h))
            def _(b=b, other=other):
                hop_one(b, other).wait_send()
    peers(lambda o: hop_two(h, o).wait_send())
    peers(lambda o: remote(loss_head.at[h], loss_head.at[h], lh_send.at[o], lh_recv.at[h], c, o).wait_send())

    def drain(j, carry):
        for block in range(nc):
            @pl.when(block > c)
            def _(block=block):
                go_right(j, block).wait_send()

            @pl.when(block < c)
            def _(block=block):
                go_left(j, block).wait_send()

            @pl.when((block <= c) & (c < nc - 1))
            def _(block=block):
                gather_copy(j, block, 0).wait_send()

            @pl.when((block >= c) & (c > 0))
            def _(block=block):
                gather_copy(j, block, 1).wait_send()

        return carry

    lax.fori_loop(0, chunks, drain, 0)
    for p in range(npair):
        @pl.when(p != my_pair)
        def _(p=p):
            pair_copy(p).wait_send()
    for g in range(nhead):
        @pl.when(g != my_head)
        def _(g=g):
            head_copy(g).wait_send()
    for block in range(nc):
        @pl.when((block != c) | (to_h != h))
        def _(block=block):
            final_copy(block).wait_send()


def local(
    student_query, teacher_keys, teacher_values, band_span, residual_in, norm_gain,
    w_gate, w_up, w_down, teacher_feats, keep_tiles,
):
    nc, nhead, npair = (lax.axis_size(a) for a in ("ctx", "head", "pair"))
    nh = nhead * npair
    nb = nc // nh
    rows, own_cols = residual_in.shape
    sub = rows // nh
    dc, ff = w_gate.shape
    chunks = CHUNKS
    cw = ff // chunks
    kv = teacher_keys.shape[1]
    gain = lax.dynamic_slice_in_dim(
        norm_gain, lax.axis_index(("head", "pair")) * own_cols, own_cols, 0
    )
    vmem = pl.BlockSpec(memory_space=pltpu.VMEM)
    hbm = pl.BlockSpec(memory_space=pl.ANY)
    dma = lambda *shape: pltpu.SemaphoreType.DMA(shape)
    kernel = functools.partial(layer_kernel, nc, nhead, npair, chunks)
    layer_out, loss, grad = pl.pallas_call(
        kernel,
        out_shape=(
            jax.ShapeDtypeStruct((rows, own_cols), BF16),
            jax.ShapeDtypeStruct((8, TILE), F32),
            jax.ShapeDtypeStruct((rows, own_cols), F32),
        ),
        in_specs=[vmem] * 6 + [hbm] * 3 + [vmem] * 2,
        out_specs=(vmem, vmem, vmem),
        scratch_shapes=[
            pltpu.VMEM((dc, ff), BF16),
            pltpu.VMEM((dc, ff), BF16),
            pltpu.VMEM((ff, dc), BF16),
            pltpu.VMEM((nc, rows, kv), BF16),
            pltpu.VMEM((nc, rows, kv), BF16),
            pltpu.VMEM((rows, own_cols), BF16),
            pltpu.VMEM((nh, rows, TILE), F32),
            pltpu.VMEM((nb, nh, sub, dc), BF16),
            pltpu.VMEM((nc, nh, sub, dc), BF16),
            pltpu.VMEM((nc, rows, 2 * cw), F32),
            pltpu.VMEM((chunks, nc, rows, 2 * cw), BF16),
            pltpu.VMEM((chunks, nc, rows, 2 * cw), BF16),
            pltpu.VMEM((chunks, nc, rows, 2 * cw), BF16),
            pltpu.VMEM((chunks, rows, 2 * cw), F32),
            pltpu.VMEM((chunks, nc, rows, 3 * cw), BF16),
            pltpu.VMEM((nc, rows, dc), F32),
            pltpu.VMEM((nc, rows, dc), F32),
            pltpu.VMEM((rows, ff), BF16),
            pltpu.VMEM((npair, nhead, nc, 2, sub, dc), BF16),
            pltpu.VMEM((npair, nhead, nc, 2, sub, dc), BF16),
            pltpu.VMEM((nhead, nc, 2, sub, dc), BF16),
            pltpu.VMEM((nb, nh, 2, sub, dc), BF16),
            pltpu.VMEM((nh, rows, TILE), F32),
            pltpu.VMEM((nh, 8, TILE), F32),
            pltpu.VMEM((nc, 8, TILE), F32),
            pltpu.VMEM((rows, cw), F32),
            dma(3),
            dma(2, nc), dma(2, nc),
            dma(nh), dma(nh),
            dma(nb, nh), dma(nc),
            dma(nh), dma(nh),
            dma(chunks, nc), dma(chunks, nc), dma(chunks, nc),
            dma(2, chunks, nc), dma(chunks, nc),
            dma(npair), dma(npair),
            dma(nhead), dma(nhead),
            dma(nc), dma(nb, nh),
            dma(nh), dma(nh),
            dma(nh), dma(nh),
            dma(nc), dma(nc),
        ],
        compiler_params=pltpu.CompilerParams(
            collective_id=0, has_side_effects=True, vmem_limit_bytes=60 * 1024 * 1024
        ),
        cost_estimate=pl.CostEstimate(
            flops=10 * nc * rows * dc * ff, bytes_accessed=6 * dc * ff, transcendentals=0
        ),
    )(
        student_query, teacher_keys, teacher_values, band_span.reshape(rows, 1), residual_in,
        gain.reshape(1, own_cols), w_gate, w_up, w_down, teacher_feats, keep_tiles,
    )
    return (layer_out, loss[0, :1], grad)


def solution(mesh):
    in_specs = (
        P(("groups", "ctx"), ("head", "pair")),
        P(("groups", "ctx"), ("head", "pair")),
        P(("groups", "ctx"), ("head", "pair")),
        P(("groups", "ctx")),
        P(("groups", "ctx"), ("head", "pair")),
        P(),
        P("ctx", ("head", "pair")),
        P("ctx", ("head", "pair")),
        P(("head", "pair"), "ctx"),
        P(("groups", "ctx"), ("head", "pair")),
        P(("groups", "ctx"), ("head", "pair")),
    )
    out_specs = (
        P(("groups", "ctx"), ("head", "pair")),
        P("groups"),
        P(("groups", "ctx"), ("head", "pair")),
    )
    return jax.shard_map(local, mesh=mesh, in_specs=in_specs, out_specs=out_specs, check_vma=False)
```

time: 414 us -> 269 us (0.65)
  Pallas kernels: 0 us -> 257 us
  waiting for transfers between devices: 235 us -> 0 us
  blocking collectives: 107 us -> 0 us
  matrix products: 26.1 us -> 0 us
  between operations: 17.6 us -> 0.65 us
  starting transfers between devices: 11.9 us -> 0 us
  other arithmetic: 8.81 us -> 0 us
    pallas_call x0 -> x1, Pallas kernels: none -> 257 us  [local(): pl.pallas_call(kernel, out_shape=(jax.ShapeDtypeStruct((rows, own_cols),...]
    all_gather x4 -> x0, waiting for transfers between devices: 131 us -> none  [the longest x1 40.7 us: local(): all_gate = lax.all_gather(grad_gate, 'ctx', axis=0, tiled=True)]
    reduce_scatter x3 -> x0, waiting for transfers between devices: 103 us -> none  [the longest x1 59.7 us: local(): lax.psum_scatter(partial, 'ctx', scatter_dimension=0, tiled=True)]
    psum x3 -> x0, blocking collectives: 46.1 us -> none  [the longest x1 32.8 us: local(): lax.psum((loss_part, count_part), ('ctx', 'head', 'pair'))]
    all_to_all x2 -> x0, blocking collectives: 44.3 us -> none  [the longest x1 30.7 us: local(): rows = lax.all_to_all(wide, 'ctx', split_axis=1, concat_axis=0, tiled=True)]
    dot_general x13 -> x0, matrix products: 24.6 us -> none  [the longest x1 5.65 us: local(): lax.dot_general(all_up, w_up, contract, preferred_element_type=jnp.float32)]
    all_gather x1 -> x0, blocking collectives: 16.7 us -> none  [local(): all_kv = lax.all_gather(paired, 'ctx', axis=0, tiled=True)]
    all_to_all x3 -> x0, starting transfers between devices: 11.4 us -> none  [the longest x2 6.82 us: own_sum(): lax.all_to_all(byctx, ('head', 'pair'), split_axis=0, concat_axis=2, tile...]
  transfers between devices with their start and end apart: 10 -> 0, of which waited for: 7 -> 0; matrix products, arithmetic and copies ran while one was open for 4% -> 0% of each run, Pallas kernels for 0% -> 0%
where the time goes in v2:
time: 269 us; the launch traced here: 266 us
  Pallas kernels  257 us (96%)
  local copies, waits for them, and re-layouts  8.83 us (3%)
    pallas_call x1, Pallas kernels, local(): pl.pallas_call(kernel, out_shape=(jax.ShapeDtypeStruct((rows, own_cols),...  257 us

profile of v2, /device:TPU:0, one launch (start us, length us, event | category | flops | bytes accessed | tf_op | source)
XLA Modules:
  0.0 266.5 jit_solution(2948983159623671895)
XLA Ops:
  0.6 1.3 dynamic_slice.3
  1.9 1.4 copy.14.span_ref
  3.3 1.4 copy.15.keep_ref
  4.7 257.0 %shard_map.130 = (bf16[128,1024]{1,0:T(8,128)(2,1)}, f32[8,128]{1,0:T(8,128)}, f32[128,1024]{1,0:T(8,128)}) custom-call(bf16[128,1024]{1,0:T(8,128)(2,1)} %q_ref.1, bf16[128,256]{1,0:T(8,128)(2,1)} %k_ref.1, bf16[128,256]{1,0:T(8,128)(2,1)} %v_ref.1, s32[128,1]{1,0:T(8,128)} %copy.14.span_ref, bf16[128,1024]{1,0:T(8,128)(2,1)} %res_ref.1, ...), custom_call_target="tpu_custom_call" | custom-call | flops 9395240960 | bytes 11010048 | tf_op jit(solution)/shard_map/pallas_call | solution.py:562
  261.8 1.2 slice.3
  262.9 1.7 copy.18
  264.6 1.9 copy.19

commit v3 on v2

--- a/solution.py
+++ b/solution.py
@@ -87,10 +87,12 @@
                 copy.start()
             kbuf[other] = jnp.zeros_like(k_ref)
             vbuf[other] = jnp.zeros_like(v_ref)
-    tile_count = keep_ref.shape[1]
+    tile_count = keep_ref.shape[0]
+    own_cols = res_ref.shape[1]
+    gain_own = gain_ref[:, pl.ds(pl.multiple_of(h * own_cols, TILE), own_cols)]
     for t in range(tile_count):
-        keep_wide[:, t * TILE : (t + 1) * TILE] = jnp.broadcast_to(
-            keep_ref[:, t : t + 1].astype(F32), (rows, TILE)
+        keep_wide[:, t * TILE : (t + 1) * TILE] = jnp.transpose(
+            jnp.broadcast_to(keep_ref[t : t + 1, :].astype(F32), (TILE, rows))
         ).astype(BF16)
     for other in range(nc):
         @pl.when(other < c)
@@ -98,11 +100,13 @@
             for copy in kv_copies(other, c):
                 copy.wait_recv()
 
+    span_of = jnp.transpose(jnp.broadcast_to(span_ref[...].astype(F32), (TILE, rows)))[:, :1]
+    span_of = span_of.astype(jnp.int32)
     span = nc * rows
     key_pos = lax.broadcasted_iota(jnp.int32, (rows, span), 1)
     query_pos = c * rows + lax.broadcasted_iota(jnp.int32, (rows, span), 0)
     distance = query_pos - key_pos
-    allowed = (distance >= 0) & (distance < span_ref[...])
+    allowed = (distance >= 0) & (distance < span_of)
     kv_heads = k_ref.shape[1] // HEAD_DIM
     heads = q_ref.shape[1] // HEAD_DIM
     per = heads // kv_heads
@@ -144,7 +148,7 @@
     )
     rms = jnp.sqrt(exchange(squares, sq_send, sq_recv)[:, :1] / width + 1e-05)
 
-    normed = (resid[...].astype(F32) / rms * gain_ref[...]).astype(BF16)
+    normed = (resid[...].astype(F32) / rms * gain_own).astype(BF16)
     for b in range(nb):
         nbuf[b] = normed[:, b * dc : (b + 1) * dc].reshape(nh, sub, dc)
 
@@ -199,40 +203,44 @@
     def go_left(j, dest):
         return rs_copy(j, dest, lax.rem(c + nc - 1, nc), fromright, left_recv)
 
-    def multiply(j, carry):
-        def block(i, inner_carry):
-            x = xall[i].reshape(rows, dc)
-            tmp[i, :, 0:cw] = jnp.dot(x, wg[:, cols_of(j)], preferred_element_type=F32)
-            tmp[i, :, cw : 2 * cw] = jnp.dot(x, wu[:, cols_of(j)], preferred_element_type=F32)
-            part[j, i] = tmp[i].astype(BF16)
-            return inner_carry
-
-        lax.fori_loop(0, nc, block, 0)
+    group = min(nc, 4)
+
+    def multiply(j):
+        def block(i, carry):
+            at = pl.ds(i * group, group)
+            x = xall[at].reshape(group * rows, dc)
+            for k, w in enumerate((wg, wu)):
+                cols = slice(k * cw, (k + 1) * cw)
+                y = jnp.dot(x, w[:, cols_of(j)], preferred_element_type=F32)
+                tmp[at, :, cols] = y.reshape(group, rows, cw)
+                part[j, at, :, cols] = y.astype(BF16).reshape(group, rows, cw)
+            return carry
+
+        lax.fori_loop(0, nc // group, block, 0)
         own[j] = tmp[c]
-        for dest in range(nc - 1, 0, -1):
+        for far in range(nc - 1):
             @pl.when(c == 0)
-            def _(dest=dest):
-                go_right(j, dest).start()
-        for dest in range(nc - 1):
+            def _(far=far):
+                go_right(j, nc - 1 - far).start()
+
             @pl.when(c == nc - 1)
-            def _(dest=dest):
-                go_left(j, dest).start()
-        return carry
-
-    lax.fori_loop(0, chunks, multiply, 0)
-
-    def reduce_on(j):
-        for far in range(nc - 1):
+            def _(far=far):
+                go_left(j, far).start()
+
+    def reduce_right(j):
+        for far in range(nc - 2):
             dest = nc - 1 - far
 
-            @pl.when((c > 0) & (c < dest))
+            @pl.when(c < dest)
             def _(dest=dest):
                 go_right(j, dest).wait_recv()
                 part[j, dest] = (part[j, dest].astype(F32) + fromleft[j, dest].astype(F32)).astype(BF16)
                 go_right(j, dest).start()
 
-            @pl.when((c < nc - 1) & (c > far))
-            def _(dest=far):
+    def reduce_left(j):
+        for dest in range(nc - 2):
+            @pl.when(c > dest)
+            def _(dest=dest):
                 go_left(j, dest).wait_recv()
                 part[j, dest] = (part[j, dest].astype(F32) + fromright[j, dest].astype(F32)).astype(BF16)
                 go_left(j, dest).start()
@@ -278,25 +286,24 @@
         def _():
             gather_copy(j, c, 1).start()
 
-    def forward(j):
-        for far in range(1, nc):
-            @pl.when(c >= far)
-            def _(far=far):
-                block = lax.rem(c - far + nc, nc)
-                gather_copy(j, block, 0).wait_recv()
-
-                @pl.when(c < nc - 1)
-                def _():
-                    gather_copy(j, block, 0).start()
-
-            @pl.when(c + far < nc)
-            def _(far=far):
-                block = lax.rem(c + far, nc)
-                gather_copy(j, block, 1).wait_recv()
-
-                @pl.when(c > 0)
-                def _():
-                    gather_copy(j, block, 1).start()
+    def forward(j, far):
+        @pl.when(c >= far)
+        def _():
+            block = lax.rem(c - far + nc, nc)
+            gather_copy(j, block, 0).wait_recv()
+
+            @pl.when(c < nc - 1)
+            def _():
+                gather_copy(j, block, 0).start()
+
+        @pl.when(c + far < nc)
+        def _():
+            block = lax.rem(c + far, nc)
+            gather_copy(j, block, 1).wait_recv()
+
+            @pl.when(c > 0)
+            def _():
+                gather_copy(j, block, 1).start()
 
     contract = (((1,), (1,)), ((), ()))
     acc_down[...] = jnp.zeros_like(acc_down)
@@ -304,34 +311,45 @@
 
     def accumulate(j):
         def block(i, carry):
-            hidden = gathered[j, i, :, 0:cw]
-            grad_gate = gathered[j, i, :, cw : 2 * cw]
-            grad_up = gathered[j, i, :, 2 * cw : 3 * cw]
-            acc_down[i] += jnp.dot(hidden, wd[cols_of(j), :], preferred_element_type=F32)
-            acc_grad[i] += lax.dot_general(
-                grad_gate, wg[:, cols_of(j)], contract, preferred_element_type=F32
-            ) + lax.dot_general(grad_up, wu[:, cols_of(j)], contract, preferred_element_type=F32)
+            at = pl.ds(i * group, group)
+
+            def rows_of(k):
+                return gathered[j, at, :, k * cw : (k + 1) * cw].reshape(group * rows, cw)
+
+            down = jnp.dot(rows_of(0), wd[cols_of(j), :], preferred_element_type=F32)
+            acc_down[at] += down.reshape(group, rows, dc)
+            grad = lax.dot_general(
+                rows_of(1), wg[:, cols_of(j)], contract, preferred_element_type=F32
+            ) + lax.dot_general(rows_of(2), wu[:, cols_of(j)], contract, preferred_element_type=F32)
+            acc_grad[at] += grad.reshape(group, rows, dc)
             return carry
 
-        lax.fori_loop(0, nc, block, 0)
+        lax.fori_loop(0, nc // group, block, 0)
+
+    ahead = 2
+    feature_lag = max(nc - 2, 1)
+    inside = (c > 0) & (c < nc - 1)
 
     def step(i, carry):
-        @pl.when(i < chunks)
-        def _():
-            reduce_on(i)
-
-        @pl.when((i >= 1) & (i < chunks + 1))
-        def _():
-            features(i - 1)
-
-        @pl.when(i >= 2)
-        def _():
-            forward(i - 2)
-            accumulate(i - 2)
-
+        def when(lag, body, also=True):
+            j = i - lag
+
+            @pl.when((j >= 0) & (j < chunks) & also)
+            def _():
+                body(j)
+
+        when(-ahead, multiply)
+        when(c - 1, reduce_right, inside)
+        when(nc - 2 - c, reduce_left, inside)
+        when(feature_lag, features)
+        for far in range(1, nc):
+            when(feature_lag + far, functools.partial(forward, far=far))
+        when(feature_lag + nc - 1, accumulate)
         return carry
 
-    lax.fori_loop(0, chunks + 2, step, 0)
+    for j in range(ahead):
+        multiply(j)
+    lax.fori_loop(0, chunks + feature_lag + nc - 1, step, 0)
 
     loss_part = jnp.sum(jnp.sum(loss_acc[...], axis=1, keepdims=True), axis=0, keepdims=True)
     count_part = jnp.sum(
@@ -460,7 +478,7 @@
         out_ref[:, cols] = (resid[:, cols].astype(F32) + down).astype(BF16)
         grad_norm = final[b, :, 1].reshape(rows, dc).astype(F32)
         inner_part += jnp.sum(
-            gain_ref[:, cols] * grad_norm * resid[:, cols].astype(F32), axis=1, keepdims=True
+            gain_own[:, cols] * grad_norm * resid[:, cols].astype(F32), axis=1, keepdims=True
         )
     inner[h] = jnp.broadcast_to(inner_part, (rows, TILE))
     inner_sum = exchange(inner, in_send, in_recv)[:, :1]
@@ -472,7 +490,7 @@
         cols = slice(b * dc, (b + 1) * dc)
         grad_norm = final[b, :, 1].reshape(rows, dc).astype(F32)
         grad_ref[:, cols] = (
-            gain_ref[:, cols] * grad_norm / rms - resid[:, cols].astype(F32) * scale
+            gain_own[:, cols] * grad_norm / rms - resid[:, cols].astype(F32) * scale
         )
 
     for other in range(nc):
@@ -482,7 +500,7 @@
     total = loss_ctx[0]
     for other in range(1, nc):
         total = total + loss_ctx[other]
-    loss_ref[...] = jnp.broadcast_to(total[0:1] / total[1:2], (8, TILE))
+    loss_ref[...] = total[0:1, 0:1] / total[1:2, 0:1]
 
     for other in range(nc):
         @pl.when(other > c)
@@ -552,9 +570,6 @@
     chunks = CHUNKS
     cw = ff // chunks
     kv = teacher_keys.shape[1]
-    gain = lax.dynamic_slice_in_dim(
-        norm_gain, lax.axis_index(("head", "pair")) * own_cols, own_cols, 0
-    )
     vmem = pl.BlockSpec(memory_space=pltpu.VMEM)
     hbm = pl.BlockSpec(memory_space=pl.ANY)
     dma = lambda *shape: pltpu.SemaphoreType.DMA(shape)
@@ -563,7 +578,7 @@
         kernel,
         out_shape=(
             jax.ShapeDtypeStruct((rows, own_cols), BF16),
-            jax.ShapeDtypeStruct((8, TILE), F32),
+            jax.ShapeDtypeStruct((1, 1), F32),
             jax.ShapeDtypeStruct((rows, own_cols), F32),
         ),
         in_specs=[vmem] * 6 + [hbm] * 3 + [vmem] * 2,
@@ -616,10 +631,10 @@
             flops=10 * nc * rows * dc * ff, bytes_accessed=6 * dc * ff, transcendentals=0
         ),
     )(
-        student_query, teacher_keys, teacher_values, band_span.reshape(rows, 1), residual_in,
-        gain.reshape(1, own_cols), w_gate, w_up, w_down, teacher_feats, keep_tiles,
+        student_query, teacher_keys, teacher_values, band_span.reshape(1, rows), residual_in,
+        norm_gain.reshape(1, -1), w_gate, w_up, w_down, teacher_feats, keep_tiles.T,
     )
-    return (layer_out, loss[0, :1], grad)
+    return (layer_out, loss.reshape(1), grad)
 
 
 def solution(mesh):

time: 269 us -> 233 us (0.87)
  Pallas kernels: 257 us -> 224 us
  local copies, waits for them, and re-layouts: 8.83 us -> 3.56 us
    pallas_call x1, Pallas kernels: 257 us -> 224 us  [local(): pl.pallas_call(kernel, out_shape=(jax.ShapeDtypeStruct((rows, own_cols),...]
where the time goes in v3:
time: 233 us; the launch traced here: 230 us
  Pallas kernels  224 us (96%)
  local copies, waits for them, and re-layouts  3.56 us (2%)
  between operations  2.33 us (1%)
    pallas_call x1, Pallas kernels, local(): pl.pallas_call(kernel, out_shape=(jax.ShapeDtypeStruct((rows, own_cols),...  224 us

profile of v3, /device:TPU:0, one launch (start us, length us, event | category | flops | bytes accessed | tf_op | source)
XLA Modules:
  0.0 230.0 jit_solution(5376207245488298511)
XLA Ops:
  0.6 224.1 %shard_map.130 = (bf16[128,1024]{1,0:T(8,128)(2,1)}, f32[1,1]{1,0:T(1,128)}, f32[128,1024]{1,0:T(8,128)}) custom-call(bf16[128,1024]{1,0:T(8,128)(2,1)} %q_ref.1, bf16[128,256]{1,0:T(8,128)(2,1)} %k_ref.1, bf16[128,256]{1,0:T(8,128)(2,1)} %v_ref.1, s32[1,128]{1,0:T(1,128)} %bitcast.6, bf16[128,1024]{1,0:T(8,128)(2,1)} %res_ref.1, f32[1,4096]{1,0:T(1,128)} %bitcast.4, ...), custom_call_target="tpu_custom_call" | custom-call | flops 9395240960 | bytes 11010048 | tf_op jit(solution)/shard_map/pallas_call | solution.py:577
  224.7 1.7 copy.17
  227.0 1.9 copy.19

commit v4 on v3

--- a/solution.py
+++ b/solution.py
@@ -21,9 +21,9 @@
     q_ref, k_ref, v_ref, span_ref, res_ref, gain_ref, wg_hbm, wu_hbm, wd_hbm, feats_ref, keep_ref,
     out_ref, loss_ref, grad_ref,
     wg, wu, wd, kbuf, vbuf, resid, squares, nbuf, xall, tmp, part, fromleft, fromright, own,
-    gathered, acc_down, acc_grad, keep_wide, sums, pair_in, head_in, final, inner, loss_head,
+    gathered, acc_down, acc_grad, feats, keeps, terms, sums, pair_in, head_in, final, inner, loss_head,
     loss_ctx, loss_acc,
-    w_sem, kv_send, kv_recv, sq_send, sq_recv, n_send, n_recv, x_send, x_recv, rs_send, right_recv,
+    w_sem, kv_send, kv_recv, sq_send, sq_recv, n_send, n_recv, x_send, m_send, x_recv, ft_send, ft_recv, kp_send, kp_recv, rs_send, right_recv,
     left_recv, ag_send, ag_recv, p_send, p_recv, h_send, h_recv, f_send, f_recv, in_send, in_recv,
     lh_send, lh_recv, lc_send, lc_recv,
 ):
@@ -87,18 +87,57 @@
                 copy.start()
             kbuf[other] = jnp.zeros_like(k_ref)
             vbuf[other] = jnp.zeros_like(v_ref)
-    tile_count = keep_ref.shape[0]
     own_cols = res_ref.shape[1]
     gain_own = gain_ref[:, pl.ds(pl.multiple_of(h * own_cols, TILE), own_cols)]
-    for t in range(tile_count):
-        keep_wide[:, t * TILE : (t + 1) * TILE] = jnp.transpose(
-            jnp.broadcast_to(keep_ref[t : t + 1, :].astype(F32), (TILE, rows))
-        ).astype(BF16)
+    keeps[c] = keep_ref[...]
+
+    def keep_copy(block, to_c):
+        return remote(keeps.at[block], keeps.at[block], kp_send.at[to_c], kp_recv.at[block], to_c, h)
+
+    for other in range(nc):
+        @pl.when(other != c)
+        def _(other=other):
+            keep_copy(c, other).start()
+    feats[c] = feats_ref[...]
+
+    def feats_copy(block, direction):
+        to_c = lax.rem(c + 1, nc) if direction == 0 else lax.rem(c + nc - 1, nc)
+        return remote(
+            feats.at[block], feats.at[block], ft_send.at[direction, block], ft_recv.at[block], to_c, h
+        )
+
+    def feats_forward(far):
+        @pl.when(c >= far)
+        def _():
+            block = lax.rem(c - far + nc, nc)
+            feats_copy(block, 0).wait_recv()
+
+            @pl.when(c < nc - 1)
+            def _():
+                feats_copy(block, 0).start()
+
+        @pl.when(c + far < nc)
+        def _():
+            block = lax.rem(c + far, nc)
+            feats_copy(block, 1).wait_recv()
+
+            @pl.when(c > 0)
+            def _():
+                feats_copy(block, 1).start()
+
     for other in range(nc):
         @pl.when(other < c)
         def _(other=other):
             for copy in kv_copies(other, c):
                 copy.wait_recv()
+
+    @pl.when(c < nc - 1)
+    def _():
+        feats_copy(c, 0).start()
+
+    @pl.when(c > 0)
+    def _():
+        feats_copy(c, 1).start()
 
     span_of = jnp.transpose(jnp.broadcast_to(span_ref[...].astype(F32), (TILE, rows)))[:, :1]
     span_of = span_of.astype(jnp.int32)
@@ -171,23 +210,55 @@
                 xall[c, other] = nbuf[b, other]
 
     source_h = c // nb
-    for other in range(nc):
-        @pl.when((other != c) | (source_h != h))
-        def _(other=other):
+
+    def to_head(block, row_h, g):
+        return remote(
+            xall.at[block, row_h], xall.at[block, row_h], x_send.at[g, block],
+            x_recv.at[row_h, block], c, g * npair + my_pair,
+        )
+
+    def to_mate(block, row_h, p):
+        return remote(
+            xall.at[block, row_h], xall.at[block, row_h], m_send.at[p, row_h, block],
+            x_recv.at[row_h, block], c, my_head * npair + p,
+        )
+
+    def others(count, mine, body):
+        for o in range(count):
+            @pl.when(o != mine)
+            def _(o=o):
+                body(o)
+
+    for k in range(nc):
+        block = lax.rem(c + k, nc)
+
+        @pl.when((block != c) | (source_h != h))
+        def _(block=block):
             remote(
-                xall.at[other, h], xall.at[other, h], n_send.at[0, 0], n_recv.at[other],
-                other, source_h,
+                xall.at[block, h], xall.at[block, h], n_send.at[0, 0], n_recv.at[block],
+                block, source_h,
             ).wait_recv()
 
-    def hop_two(row_h, to_h):
-        return remote(
-            xall.at[:, row_h], xall.at[:, row_h], x_send.at[to_h], x_recv.at[row_h], c, to_h
-        )
-
-    peers(lambda o: hop_two(h, o).start())
+        others(nhead, my_head, lambda g: to_head(block, h, g).start())
+        others(npair, my_pair, lambda p: to_mate(block, h, p).start())
+    feats_forward(1)
+    for k in range(nc):
+        block = lax.rem(c + k, nc)
+
+        def pass_on(g):
+            row_h = g * npair + my_pair
+            to_head(block, row_h, g).wait_recv()
+            others(npair, my_pair, lambda p: to_mate(block, row_h, p).start())
+
+        others(nhead, my_head, pass_on)
     for copy in weight_copies:
         copy.wait()
-    peers(lambda o: hop_two(o, o).wait_recv())
+    for k in range(nc):
+        for g in range(nhead):
+            others(
+                npair, my_pair, lambda p: to_mate(k, g * npair + p, p).wait_recv()
+            )
+    others(nc, c, lambda o: keep_copy(o, o).wait_recv())
 
     def cols_of(j):
         return pl.ds(pl.multiple_of(j * cw, cw), cw)
@@ -253,6 +324,18 @@
         )
 
     loss_acc[...] = jnp.zeros_like(loss_acc)
+    per_chunk = cw // TILE
+
+    def keep_of(j, block):
+        wide = [
+            jnp.transpose(
+                jnp.broadcast_to(
+                    keeps[block, pl.ds(j * per_chunk + t, 1), :].astype(F32), (TILE, rows)
+                )
+            )
+            for t in range(per_chunk)
+        ]
+        return jnp.concatenate(wide, axis=1) if per_chunk > 1 else wide[0]
 
     def features(j):
         @pl.when(c > 0)
@@ -270,13 +353,9 @@
         lifted = jnp.maximum(gate, 0.0)
         squared = lifted * lifted
         act = squared * up
-        keep = keep_wide[:, cols_of(j)].astype(F32)
         differ = act - feats_ref[:, cols_of(j)].astype(F32)
-        grad_act = keep * differ
-        loss_acc[...] += grad_act * differ
-        gathered[j, c, :, 0:cw] = act.astype(BF16)
-        gathered[j, c, :, cw : 2 * cw] = (grad_act * up * 2.0 * lifted).astype(BF16)
-        gathered[j, c, :, 2 * cw : 3 * cw] = (grad_act * squared).astype(BF16)
+        loss_acc[...] += keep_of(j, c) * differ * differ
+        gathered[j, c] = own[j].astype(BF16)
 
         @pl.when(c < nc - 1)
         def _():
@@ -310,11 +389,26 @@
     acc_grad[...] = jnp.zeros_like(acc_grad)
 
     def accumulate(j):
+        def derive(i, carry):
+            gate = gathered[j, i, :, 0:cw].astype(F32)
+            up = gathered[j, i, :, cw : 2 * cw].astype(F32)
+            lifted = jnp.maximum(gate, 0.0)
+            squared = lifted * lifted
+            act = squared * up
+            differ = act - feats[i, :, cols_of(j)].astype(F32)
+            grad_act = keep_of(j, i) * differ
+            terms[0, i] = act.astype(BF16)
+            terms[1, i] = (grad_act * up * 2.0 * lifted).astype(BF16)
+            terms[2, i] = (grad_act * squared).astype(BF16)
+            return carry
+
+        lax.fori_loop(0, nc, derive, 0)
+
         def block(i, carry):
             at = pl.ds(i * group, group)
 
             def rows_of(k):
-                return gathered[j, at, :, k * cw : (k + 1) * cw].reshape(group * rows, cw)
+                return terms[k, at].reshape(group * rows, cw)
 
             down = jnp.dot(rows_of(0), wd[cols_of(j), :], preferred_element_type=F32)
             acc_down[at] += down.reshape(group, rows, dc)
@@ -337,6 +431,10 @@
             @pl.when((j >= 0) & (j < chunks) & also)
             def _():
                 body(j)
+
+        @pl.when(i < nc - 2)
+        def _():
+            feats_forward(i + 2)
 
         when(-ahead, multiply)
         when(c - 1, reduce_right, inside)
@@ -359,57 +457,35 @@
     loss_head[h] = jnp.where(line == 0, loss_part, count_part)
     peers(lambda o: remote(loss_head.at[h], loss_head.at[h], lh_send.at[o], lh_recv.at[h], c, o).start())
 
-    for p in range(npair):
-        for g in range(nhead):
-            o = g * npair + p
-            for i in range(nc):
-                sums[p, g, i, 0] = acc_down[i, o * sub : (o + 1) * sub].astype(BF16)
-                sums[p, g, i, 1] = acc_grad[i, o * sub : (o + 1) * sub].astype(BF16)
-
-    def pair_copy(p):
-        return remote(
-            sums.at[p], pair_in.at[my_pair], p_send.at[p], p_recv.at[my_pair], c, my_head * npair + p
-        )
-
-    def pair_wait(p):
-        return remote(
-            sums.at[p], pair_in.at[p], p_send.at[p], p_recv.at[p], c, my_head * npair + p
-        )
-
-    for p in range(npair):
-        @pl.when(p != my_pair)
-        def _(p=p):
-            pair_copy(p).start()
-    for p in range(npair):
-        @pl.when(p != my_pair)
-        def _(p=p):
-            pair_wait(p).wait_recv()
-
-            def add(i, carry):
-                g, k = i // nc, i % nc
-                sums[my_pair, g, k] = (
-                    sums[my_pair, g, k].astype(F32) + pair_in[p, g, k].astype(F32)
-                ).astype(BF16)
-                return carry
-
-            lax.fori_loop(0, nhead * nc, add, 0)
-
-    def head_copy(g):
-        return remote(
-            sums.at[my_pair, g], head_in.at[my_head], h_send.at[g], h_recv.at[my_head],
+    def pair_copy(p, k, slot):
+        return remote(
+            sums.at[p, k], pair_in.at[slot, k], p_send.at[p, k], p_recv.at[slot, k],
+            c, my_head * npair + p,
+        )
+
+    for k in range(nc):
+        for p in range(npair):
+            for g in range(nhead):
+                o = g * npair + p
+                sums[p, k, g, 0] = acc_down[k, o * sub : (o + 1) * sub].astype(BF16)
+                sums[p, k, g, 1] = acc_grad[k, o * sub : (o + 1) * sub].astype(BF16)
+        others(npair, my_pair, lambda p: pair_copy(p, k, my_pair).start())
+
+    def head_copy(g, k, slot):
+        return remote(
+            sums.at[my_pair, k, g], head_in.at[slot, k], h_send.at[g, k], h_recv.at[slot, k],
             c, g * npair + my_pair,
         )
 
-    def head_wait(g):
-        return remote(
-            sums.at[my_pair, g], head_in.at[g], h_send.at[g], h_recv.at[g],
-            c, g * npair + my_pair,
-        )
-
-    for g in range(nhead):
-        @pl.when(g != my_head)
-        def _(g=g):
-            head_copy(g).start()
+    for k in range(nc):
+        def add_pair(p):
+            pair_copy(p, k, p).wait_recv()
+            sums[my_pair, k] = (
+                sums[my_pair, k].astype(F32) + pair_in[p, k].astype(F32)
+            ).astype(BF16)
+
+        others(npair, my_pair, add_pair)
+        others(nhead, my_head, lambda g: head_copy(g, k, my_head).start())
 
     peers(lambda o: remote(loss_head.at[o], loss_head.at[o], lh_send.at[o], lh_recv.at[o], c, o).wait_recv())
     head_total = loss_head[0]
@@ -427,29 +503,23 @@
         def _(other=other):
             loss_copy(c, other).start()
 
-    for g in range(nhead):
-        @pl.when(g != my_head)
-        def _(g=g):
-            head_wait(g).wait_recv()
-
-            def add(k, carry):
-                sums[my_pair, my_head, k] = (
-                    sums[my_pair, my_head, k].astype(F32) + head_in[g, k].astype(F32)
-                ).astype(BF16)
-                return carry
-
-            lax.fori_loop(0, nc, add, 0)
-
     to_h = c // nb
     slot = lax.rem(c, nb) if nb > 1 else 0
 
     def final_copy(block):
         return remote(
-            sums.at[my_pair, my_head, block], final.at[slot, h], f_send.at[block],
+            sums.at[my_pair, block, my_head], final.at[slot, h], f_send.at[block],
             f_recv.at[slot, h], block, to_h,
         )
 
     for block in range(nc):
+        def add_head(g):
+            head_copy(g, block, g).wait_recv()
+            sums[my_pair, block, my_head] = (
+                sums[my_pair, block, my_head].astype(F32) + head_in[g, block].astype(F32)
+            ).astype(BF16)
+
+        others(nhead, my_head, add_head)
         mine = (block == c) & (to_h == h)
 
         @pl.when(jnp.logical_not(mine))
@@ -458,7 +528,7 @@
 
         @pl.when(mine)
         def _(block=block):
-            final[slot, h] = sums[my_pair, my_head, block]
+            final[slot, h] = sums[my_pair, block, my_head]
 
     for b in range(nb):
         for other in range(nh):
@@ -519,7 +589,20 @@
             @pl.when((h * nb + b != c) | (other != h))
             def _(b=b, other=other):
                 hop_one(b, other).wait_send()
-    peers(lambda o: hop_two(h, o).wait_send())
+    for block in range(nc):
+        others(nhead, my_head, lambda g: to_head(block, h, g).wait_send())
+        for g in range(nhead):
+            others(npair, my_pair, lambda p: to_mate(block, g * npair + my_pair, p).wait_send())
+
+        @pl.when((block <= c) & (c < nc - 1))
+        def _(block=block):
+            feats_copy(block, 0).wait_send()
+
+        @pl.when((block >= c) & (c > 0))
+        def _(block=block):
+            feats_copy(block, 1).wait_send()
+
+    others(nc, c, lambda o: keep_copy(c, o).wait_send())
     peers(lambda o: remote(loss_head.at[h], loss_head.at[h], lh_send.at[o], lh_recv.at[h], c, o).wait_send())
 
     def drain(j, carry):
@@ -543,14 +626,9 @@
         return carry
 
     lax.fori_loop(0, chunks, drain, 0)
-    for p in range(npair):
-        @pl.when(p != my_pair)
-        def _(p=p):
-            pair_copy(p).wait_send()
-    for g in range(nhead):
-        @pl.when(g != my_head)
-        def _(g=g):
-            head_copy(g).wait_send()
+    for k in range(nc):
+        others(npair, my_pair, lambda p: pair_copy(p, k, my_pair).wait_send())
+        others(nhead, my_head, lambda g: head_copy(g, k, my_head).wait_send())
     for block in range(nc):
         @pl.when((block != c) | (to_h != h))
         def _(block=block):
@@ -598,12 +676,14 @@
             pltpu.VMEM((chunks, nc, rows, 2 * cw), BF16),
             pltpu.VMEM((chunks, nc, rows, 2 * cw), BF16),
             pltpu.VMEM((chunks, rows, 2 * cw), F32),
-            pltpu.VMEM((chunks, nc, rows, 3 * cw), BF16),
+            pltpu.VMEM((chunks, nc, rows, 2 * cw), BF16),
             pltpu.VMEM((nc, rows, dc), F32),
             pltpu.VMEM((nc, rows, dc), F32),
-            pltpu.VMEM((rows, ff), BF16),
-            pltpu.VMEM((npair, nhead, nc, 2, sub, dc), BF16),
-            pltpu.VMEM((npair, nhead, nc, 2, sub, dc), BF16),
+            pltpu.VMEM((nc, rows, ff), BF16),
+            pltpu.VMEM((nc, ff // TILE, rows), jnp.int32),
+            pltpu.VMEM((3, nc, rows, cw), BF16),
+            pltpu.VMEM((npair, nc, nhead, 2, sub, dc), BF16),
+            pltpu.VMEM((npair, nc, nhead, 2, sub, dc), BF16),
             pltpu.VMEM((nhead, nc, 2, sub, dc), BF16),
             pltpu.VMEM((nb, nh, 2, sub, dc), BF16),
             pltpu.VMEM((nh, rows, TILE), F32),
@@ -614,11 +694,13 @@
             dma(2, nc), dma(2, nc),
             dma(nh), dma(nh),
             dma(nb, nh), dma(nc),
-            dma(nh), dma(nh),
+            dma(nhead, nc), dma(npair, nh, nc), dma(nh, nc),
+            dma(2, nc), dma(nc),
+            dma(nc), dma(nc),
             dma(chunks, nc), dma(chunks, nc), dma(chunks, nc),
             dma(2, chunks, nc), dma(chunks, nc),
-            dma(npair), dma(npair),
-            dma(nhead), dma(nhead),
+            dma(npair, nc), dma(npair, nc),
+            dma(nhead, nc), dma(nhead, nc),
             dma(nc), dma(nb, nh),
             dma(nh), dma(nh),
             dma(nh), dma(nh),

time: 233 us -> 200 us (0.86)
  Pallas kernels: 224 us -> 191 us
    pallas_call x1, Pallas kernels: 224 us -> 191 us  [local(): pl.pallas_call(kernel, out_shape=(jax.ShapeDtypeStruct((rows, own_cols),...]
where the time goes in v4:
time: 200 us; the launch traced here: 197 us
  Pallas kernels  191 us (96%)
  local copies, waits for them, and re-layouts  3.56 us (2%)
  between operations  2.33 us (1%)
    pallas_call x1, Pallas kernels, local(): pl.pallas_call(kernel, out_shape=(jax.ShapeDtypeStruct((rows, own_cols),...  191 us

profile of v4, /device:TPU:0, one launch (start us, length us, event | category | flops | bytes accessed | tf_op | source)
XLA Modules:
  0.0 197.0 jit_solution(10892270895405135044)
XLA Ops:
  0.6 191.2 %shard_map.130 = (bf16[128,1024]{1,0:T(8,128)(2,1)}, f32[1,1]{1,0:T(1,128)}, f32[128,1024]{1,0:T(8,128)}) custom-call(bf16[128,1024]{1,0:T(8,128)(2,1)} %q_ref.1, bf16[128,256]{1,0:T(8,128)(2,1)} %k_ref.1, bf16[128,256]{1,0:T(8,128)(2,1)} %v_ref.1, s32[1,128]{1,0:T(1,128)} %bitcast.6, bf16[128,1024]{1,0:T(8,128)(2,1)} %res_ref.1, f32[1,4096]{1,0:T(1,128)} %bitcast.4, ...), custom_call_target="tpu_custom_call" | custom-call | flops 9395240960 | bytes 11010048 | tf_op jit(solution)/shard_map/pallas_call | solution.py:655
  191.8 1.7 copy.17
  194.0 1.9 copy.19

commit v5 on v4

--- a/solution.py
+++ b/solution.py
@@ -20,8 +20,8 @@
     nc, nhead, npair, chunks,
     q_ref, k_ref, v_ref, span_ref, res_ref, gain_ref, wg_hbm, wu_hbm, wd_hbm, feats_ref, keep_ref,
     out_ref, loss_ref, grad_ref,
-    wg, wu, wd, kbuf, vbuf, resid, squares, nbuf, xall, tmp, part, fromleft, fromright, own,
-    gathered, acc_down, acc_grad, feats, keeps, terms, sums, pair_in, head_in, final, inner, loss_head,
+    wg, wu, wd, kbuf, vbuf, resid, squares, nbuf, xall, tmp, part, landing, own,
+    gathered, acc_down, acc_grad, feats, keeps, wide_keep, terms, sums, pair_in, head_in, final, inner, loss_head,
     loss_ctx, loss_acc,
     w_sem, kv_send, kv_recv, sq_send, sq_recv, n_send, n_recv, x_send, m_send, x_recv, ft_send, ft_recv, kp_send, kp_recv, rs_send, right_recv,
     left_recv, ag_send, ag_recv, p_send, p_recv, h_send, h_recv, f_send, f_recv, in_send, in_recv,
@@ -29,6 +29,7 @@
 ):
     nh = nhead * npair
     nb = nc // nh
+    depth = terms.shape[0]
     rows = q_ref.shape[0]
     sub = rows // nh
     dc = wg.shape[0]
@@ -78,6 +79,15 @@
             remote(vbuf.at[block], vbuf.at[block], kv_send.at[1, to_c], kv_recv.at[1, block], to_c, h),
         )
 
+    keeps[c] = keep_ref[...]
+
+    def keep_copy(block, to_c):
+        return remote(keeps.at[block], keeps.at[block], kp_send.at[to_c], kp_recv.at[block], to_c, h)
+
+    for other in range(nc):
+        @pl.when(other != c)
+        def _(other=other):
+            keep_copy(c, other).start()
     kbuf[c] = k_ref[...]
     vbuf[c] = v_ref[...]
     for other in range(nc):
@@ -89,42 +99,46 @@
             vbuf[other] = jnp.zeros_like(v_ref)
     own_cols = res_ref.shape[1]
     gain_own = gain_ref[:, pl.ds(pl.multiple_of(h * own_cols, TILE), own_cols)]
-    keeps[c] = keep_ref[...]
-
-    def keep_copy(block, to_c):
-        return remote(keeps.at[block], keeps.at[block], kp_send.at[to_c], kp_recv.at[block], to_c, h)
+    feats[c] = feats_ref[...]
+
+    def feats_copy(block, direction):
+        to_c = lax.rem(c + 1, nc) if direction == 0 else lax.rem(c + nc - 1, nc)
+        return remote(
+            feats.at[block], feats.at[block], ft_send.at[direction, block], ft_recv.at[block], to_c, h
+        )
+
+    def feats_forward(far):
+        @pl.when(c >= far)
+        def _():
+            block = lax.rem(c - far + nc, nc)
+            feats_copy(block, 0).wait_recv()
+
+            @pl.when(c < nc - 1)
+            def _():
+                feats_copy(block, 0).start()
+
+        @pl.when(c + far < nc)
+        def _():
+            block = lax.rem(c + far, nc)
+            feats_copy(block, 1).wait_recv()
+
+            @pl.when(c > 0)
+            def _():
+                feats_copy(block, 1).start()
 
     for other in range(nc):
         @pl.when(other != c)
         def _(other=other):
-            keep_copy(c, other).start()
-    feats[c] = feats_ref[...]
-
-    def feats_copy(block, direction):
-        to_c = lax.rem(c + 1, nc) if direction == 0 else lax.rem(c + nc - 1, nc)
-        return remote(
-            feats.at[block], feats.at[block], ft_send.at[direction, block], ft_recv.at[block], to_c, h
-        )
-
-    def feats_forward(far):
-        @pl.when(c >= far)
-        def _():
-            block = lax.rem(c - far + nc, nc)
-            feats_copy(block, 0).wait_recv()
-
-            @pl.when(c < nc - 1)
-            def _():
-                feats_copy(block, 0).start()
-
-        @pl.when(c + far < nc)
-        def _():
-            block = lax.rem(c + far, nc)
-            feats_copy(block, 1).wait_recv()
-
-            @pl.when(c > 0)
-            def _():
-                feats_copy(block, 1).start()
-
+            keep_copy(other, other).wait_recv()
+
+    def widen(block, carry):
+        for t in range(ff // TILE):
+            wide_keep[block, :, t * TILE : (t + 1) * TILE] = jnp.transpose(
+                jnp.broadcast_to(keeps[block, t : t + 1, :].astype(F32), (TILE, rows))
+            ).astype(BF16)
+        return carry
+
+    lax.fori_loop(0, nc, widen, 0)
     for other in range(nc):
         @pl.when(other < c)
         def _(other=other):
@@ -258,21 +272,20 @@
             others(
                 npair, my_pair, lambda p: to_mate(k, g * npair + p, p).wait_recv()
             )
-    others(nc, c, lambda o: keep_copy(o, o).wait_recv())
 
     def cols_of(j):
         return pl.ds(pl.multiple_of(j * cw, cw), cw)
 
-    def rs_copy(j, dest, to_c, buf, recv):
-        return remote(
-            part.at[j, dest], buf.at[j, dest], rs_send.at[j, dest], recv.at[j, dest], to_c, h
+    def rs_copy(j, dest, to_c, slot, recv):
+        return remote(
+            part.at[j, dest], landing.at[j, slot], rs_send.at[j, dest], recv.at[j, dest], to_c, h
         )
 
     def go_right(j, dest):
-        return rs_copy(j, dest, lax.rem(c + 1, nc), fromleft, right_recv)
+        return rs_copy(j, dest, lax.rem(c + 1, nc), dest + 1, right_recv)
 
     def go_left(j, dest):
-        return rs_copy(j, dest, lax.rem(c + nc - 1, nc), fromright, left_recv)
+        return rs_copy(j, dest, lax.rem(c + nc - 1, nc), dest, left_recv)
 
     group = min(nc, 4)
 
@@ -289,6 +302,8 @@
 
         lax.fori_loop(0, nc // group, block, 0)
         own[j] = tmp[c]
+
+    def edge_send(j):
         for far in range(nc - 1):
             @pl.when(c == 0)
             def _(far=far):
@@ -305,7 +320,7 @@
             @pl.when(c < dest)
             def _(dest=dest):
                 go_right(j, dest).wait_recv()
-                part[j, dest] = (part[j, dest].astype(F32) + fromleft[j, dest].astype(F32)).astype(BF16)
+                part[j, dest] = (part[j, dest].astype(F32) + landing[j, dest + 1].astype(F32)).astype(BF16)
                 go_right(j, dest).start()
 
     def reduce_left(j):
@@ -313,7 +328,7 @@
             @pl.when(c > dest)
             def _(dest=dest):
                 go_left(j, dest).wait_recv()
-                part[j, dest] = (part[j, dest].astype(F32) + fromright[j, dest].astype(F32)).astype(BF16)
+                part[j, dest] = (part[j, dest].astype(F32) + landing[j, dest].astype(F32)).astype(BF16)
                 go_left(j, dest).start()
 
     def gather_copy(j, block, direction):
@@ -324,29 +339,32 @@
         )
 
     loss_acc[...] = jnp.zeros_like(loss_acc)
-    per_chunk = cw // TILE
-
     def keep_of(j, block):
-        wide = [
-            jnp.transpose(
-                jnp.broadcast_to(
-                    keeps[block, pl.ds(j * per_chunk + t, 1), :].astype(F32), (TILE, rows)
-                )
-            )
-            for t in range(per_chunk)
-        ]
-        return jnp.concatenate(wide, axis=1) if per_chunk > 1 else wide[0]
+        return wide_keep[block, :, cols_of(j)].astype(F32)
+
+    def derive(j, i):
+        gate = gathered[j, i, :, 0:cw].astype(F32)
+        up = gathered[j, i, :, cw : 2 * cw].astype(F32)
+        lifted = jnp.maximum(gate, 0.0)
+        squared = lifted * lifted
+        act = squared * up
+        differ = act - feats[i, :, cols_of(j)].astype(F32)
+        grad_act = keep_of(j, i) * differ
+        at = lax.rem(j, depth)
+        terms[at, 0, i] = act.astype(BF16)
+        terms[at, 1, i] = (grad_act * up * 2.0 * lifted).astype(BF16)
+        terms[at, 2, i] = (grad_act * squared).astype(BF16)
 
     def features(j):
         @pl.when(c > 0)
         def _():
             go_right(j, c).wait_recv()
-            own[j] = own[j] + fromleft[j, c].astype(F32)
+            own[j] = own[j] + landing[j, c + 1].astype(F32)
 
         @pl.when(c < nc - 1)
         def _():
             go_left(j, c).wait_recv()
-            own[j] = own[j] + fromright[j, c].astype(F32)
+            own[j] = own[j] + landing[j, c].astype(F32)
 
         gate = own[j, :, 0:cw]
         up = own[j, :, cw : 2 * cw]
@@ -365,6 +383,8 @@
         def _():
             gather_copy(j, c, 1).start()
 
+        derive(j, c)
+
     def forward(j, far):
         @pl.when(c >= far)
         def _():
@@ -375,6 +395,8 @@
             def _():
                 gather_copy(j, block, 0).start()
 
+            derive(j, block)
+
         @pl.when(c + far < nc)
         def _():
             block = lax.rem(c + far, nc)
@@ -384,31 +406,18 @@
             def _():
                 gather_copy(j, block, 1).start()
 
+            derive(j, block)
+
     contract = (((1,), (1,)), ((), ()))
     acc_down[...] = jnp.zeros_like(acc_down)
     acc_grad[...] = jnp.zeros_like(acc_grad)
 
     def accumulate(j):
-        def derive(i, carry):
-            gate = gathered[j, i, :, 0:cw].astype(F32)
-            up = gathered[j, i, :, cw : 2 * cw].astype(F32)
-            lifted = jnp.maximum(gate, 0.0)
-            squared = lifted * lifted
-            act = squared * up
-            differ = act - feats[i, :, cols_of(j)].astype(F32)
-            grad_act = keep_of(j, i) * differ
-            terms[0, i] = act.astype(BF16)
-            terms[1, i] = (grad_act * up * 2.0 * lifted).astype(BF16)
-            terms[2, i] = (grad_act * squared).astype(BF16)
-            return carry
-
-        lax.fori_loop(0, nc, derive, 0)
-
         def block(i, carry):
             at = pl.ds(i * group, group)
 
             def rows_of(k):
-                return terms[k, at].reshape(group * rows, cw)
+                return terms[lax.rem(j, depth), k, at].reshape(group * rows, cw)
 
             down = jnp.dot(rows_of(0), wd[cols_of(j), :], preferred_element_type=F32)
             acc_down[at] += down.reshape(group, rows, dc)
@@ -442,11 +451,13 @@
         when(feature_lag, features)
         for far in range(1, nc):
             when(feature_lag + far, functools.partial(forward, far=far))
+        when(-1, edge_send)
         when(feature_lag + nc - 1, accumulate)
         return carry
 
-    for j in range(ahead):
-        multiply(j)
+    multiply(0)
+    edge_send(0)
+    multiply(1)
     lax.fori_loop(0, chunks + feature_lag + nc - 1, step, 0)
 
     loss_part = jnp.sum(jnp.sum(loss_acc[...], axis=1, keepdims=True), axis=0, keepdims=True)
@@ -673,15 +684,15 @@
             pltpu.VMEM((nc, nh, sub, dc), BF16),
             pltpu.VMEM((nc, rows, 2 * cw), F32),
             pltpu.VMEM((chunks, nc, rows, 2 * cw), BF16),
-            pltpu.VMEM((chunks, nc, rows, 2 * cw), BF16),
-            pltpu.VMEM((chunks, nc, rows, 2 * cw), BF16),
+            pltpu.VMEM((chunks, nc + 1, rows, 2 * cw), BF16),
             pltpu.VMEM((chunks, rows, 2 * cw), F32),
             pltpu.VMEM((chunks, nc, rows, 2 * cw), BF16),
             pltpu.VMEM((nc, rows, dc), F32),
             pltpu.VMEM((nc, rows, dc), F32),
             pltpu.VMEM((nc, rows, ff), BF16),
             pltpu.VMEM((nc, ff // TILE, rows), jnp.int32),
-            pltpu.VMEM((3, nc, rows, cw), BF16),
+            pltpu.VMEM((nc, rows, ff), BF16),
+            pltpu.VMEM((min(chunks, nc), 3, nc, rows, cw), BF16),
             pltpu.VMEM((npair, nc, nhead, 2, sub, dc), BF16),
             pltpu.VMEM((npair, nc, nhead, 2, sub, dc), BF16),
             pltpu.VMEM((nhead, nc, 2, sub, dc), BF16),

time: 200 us -> 195 us (0.975); the launches traced: 197 us -> 195 us
  Pallas kernels: 191 us -> 189 us
    pallas_call x1, Pallas kernels: 191 us -> 189 us  [local(): pl.pallas_call(kernel, out_shape=(jax.ShapeDtypeStruct((rows, own_cols),...]
where the time goes in v5:
time: 195 us
  Pallas kernels  189 us (97%)
  local copies, waits for them, and re-layouts  3.56 us (2%)
  between operations  2.33 us (1%)
    pallas_call x1, Pallas kernels, local(): pl.pallas_call(kernel, out_shape=(jax.ShapeDtypeStruct((rows, own_cols),...  189 us

profile of v5, /device:TPU:0, one launch (start us, length us, event | category | flops | bytes accessed | tf_op | source)
XLA Modules:
  0.0 194.7 jit_solution(1675324288997171997)
XLA Ops:
  0.6 188.8 %shard_map.130 = (bf16[128,1024]{1,0:T(8,128)(2,1)}, f32[1,1]{1,0:T(1,128)}, f32[128,1024]{1,0:T(8,128)}) custom-call(bf16[128,1024]{1,0:T(8,128)(2,1)} %q_ref.1, bf16[128,256]{1,0:T(8,128)(2,1)} %k_ref.1, bf16[128,256]{1,0:T(8,128)(2,1)} %v_ref.1, s32[1,128]{1,0:T(1,128)} %bitcast.6, bf16[128,1024]{1,0:T(8,128)(2,1)} %res_ref.1, f32[1,4096]{1,0:T(1,128)} %bitcast.4, ...), custom_call_target="tpu_custom_call" | custom-call | flops 9395240960 | bytes 11010048 | tf_op jit(solution)/shard_map/pallas_call | solution.py:666
  189.4 1.7 copy.17
  191.7 1.9 copy.19

commit v6 on v5

--- a/solution.py
+++ b/solution.py
@@ -383,8 +383,6 @@
         def _():
             gather_copy(j, c, 1).start()
 
-        derive(j, c)
-
     def forward(j, far):
         @pl.when(c >= far)
         def _():
@@ -395,8 +393,6 @@
             def _():
                 gather_copy(j, block, 0).start()
 
-            derive(j, block)
-
         @pl.when(c + far < nc)
         def _():
             block = lax.rem(c + far, nc)
@@ -406,7 +402,14 @@
             def _():
                 gather_copy(j, block, 1).start()
 
-            derive(j, block)
+    def derive_far(j, far):
+        @pl.when(c >= far)
+        def _():
+            derive(j, lax.rem(c - far + nc, nc))
+
+        @pl.when(c + far < nc)
+        def _():
+            derive(j, lax.rem(c + far, nc))
 
     contract = (((1,), (1,)), ((), ()))
     acc_down[...] = jnp.zeros_like(acc_down)
@@ -441,17 +444,21 @@
             def _():
                 body(j)
 
-        @pl.when(i < nc - 2)
-        def _():
-            feats_forward(i + 2)
-
-        when(-ahead, multiply)
         when(c - 1, reduce_right, inside)
         when(nc - 2 - c, reduce_left, inside)
         when(feature_lag, features)
         for far in range(1, nc):
             when(feature_lag + far, functools.partial(forward, far=far))
         when(-1, edge_send)
+
+        @pl.when(i < nc - 2)
+        def _():
+            feats_forward(i + 2)
+
+        when(-ahead, multiply)
+        when(feature_lag, lambda j: derive(j, c))
+        for far in range(1, nc):
+            when(feature_lag + far, functools.partial(derive_far, far=far))
         when(feature_lag + nc - 1, accumulate)
         return carry
 

time: 195 us -> 194 us (level); the launches traced: 195 us -> 191 us
  Pallas kernels: 189 us -> 185 us
    pallas_call x1, Pallas kernels: 189 us -> 185 us  [local(): pl.pallas_call(kernel, out_shape=(jax.ShapeDtypeStruct((rows, own_cols),...]
where the time goes in v6:
time: 194 us; the launch traced here: 191 us
  Pallas kernels  185 us (95%)
  local copies, waits for them, and re-layouts  3.56 us (2%)
  between operations  2.33 us (1%)
    pallas_call x1, Pallas kernels, local(): pl.pallas_call(kernel, out_shape=(jax.ShapeDtypeStruct((rows, own_cols),...  185 us

profile of v6, /device:TPU:0, one launch (start us, length us, event | category | flops | bytes accessed | tf_op | source)
XLA Modules:
  0.0 191.3 jit_solution(16923603931917855574)
XLA Ops:
  0.6 185.4 %shard_map.130 = (bf16[128,1024]{1,0:T(8,128)(2,1)}, f32[1,1]{1,0:T(1,128)}, f32[128,1024]{1,0:T(8,128)}) custom-call(bf16[128,1024]{1,0:T(8,128)(2,1)} %q_ref.1, bf16[128,256]{1,0:T(8,128)(2,1)} %k_ref.1, bf16[128,256]{1,0:T(8,128)(2,1)} %v_ref.1, s32[1,128]{1,0:T(1,128)} %bitcast.6, bf16[128,1024]{1,0:T(8,128)(2,1)} %res_ref.1, f32[1,4096]{1,0:T(1,128)} %bitcast.4, ...), custom_call_target="tpu_custom_call" | custom-call | flops 9395240960 | bytes 11010048 | tf_op jit(solution)/shard_map/pallas_call | solution.py:673
  186.0 1.7 copy.17
  188.2 1.9 copy.19
